TPU v7x, 32 devices: a whole 2x2x4 slice. The times are simulated.
32 devices in a mesh: groups: 1, grid: 32 (over z, y, x, core).
Axes of the slice: x: 2, y: 2, z: 4, core: 2. Of those that a mesh axis runs over, the one named last changes fastest.
Arguments:
- collocation: bfloat16 [512, 512, 512], P(('groups', 'grid')), may hold values from -0.25 to 0.25
- coords: float32 [512, 3, 512], P(('groups', 'grid')), may hold values from -6 to 6
- weights: float32 [512, 512], P(('groups', 'grid')), may hold values from 0.05 to 0.5
- owners: int32 [512, 16], P(('groups', 'grid')), may hold values from 0 to 31, all different within a row; in each aligned block of 16 rows (0 to 15, 16 to 31, ...) at most 8 rows name the same one
- slots: int32 [512, 16], P(('groups', 'grid')), may hold values from 0 to 31
- counts: int32 [512], P(('groups', 'grid')), may hold values from 2 to 4
- dens_tiles: bfloat16 [1024, 128, 128], P(('groups', 'grid')), may hold values from -6 to 6
- dens_scales: float32 [1024], P(('groups', 'grid')), may hold values from 0.5 to 2
- fock_prev: bfloat16 [1024, 128, 128], P(('groups', 'grid')), may hold values from -6 to 6
Outputs:
- fock: float32 [1024, 128, 128], P(('groups', 'grid'))
Inputs may be any that keep to these rules, and one draw needn't show every extreme that they name: Each batch names 16 different owners; the batches of one device name one owner at most 8 times, a bound that some block reaches.
All inputs are finite; a program needn't handle non-finite values.
Results may differ from a plain program's by a relative error of at most 0.004.
Values may be sent and summed in bfloat16 or wider, within the bound.
A program may use at most 128 MiB of HBM per device.

v0:
```python
import jax
import jax.numpy as jnp
from jax import lax
from jax.sharding import PartitionSpec as P

SOFTEN = 0.5


def point_kernel(tile_placement, quadrature_weight):
    diff = tile_placement[:, :, None] - tile_placement[:, None, :]
    dist2 = jnp.sum(diff * diff, axis=0)
    return (
        quadrature_weight[:, None] * quadrature_weight[None, :] / jnp.sqrt(dist2 + SOFTEN * SOFTEN)
    ).astype(jnp.bfloat16)


def exchange_contribution(
    collocation_matrix, density_delta, exchange_kernel, tile_width, listed_tiles
):
    projected_field = jnp.dot(
        collocation_matrix, density_delta, preferred_element_type=jnp.float32
    ).astype(jnp.bfloat16)
    grid_field = jnp.dot(
        exchange_kernel, projected_field, preferred_element_type=jnp.float32
    ).astype(jnp.bfloat16)
    full_exchange = lax.dot_general(
        collocation_matrix, grid_field, (((0,), (0,)), ((), ())), preferred_element_type=jnp.float32
    )
    return (
        full_exchange.reshape(listed_tiles, tile_width, listed_tiles, tile_width)
        .transpose(0, 2, 1, 3)
        .reshape(listed_tiles * listed_tiles, tile_width, tile_width)
    )


def shards(collocation, coords, weights, owners, slots, counts, dens_tiles, dens_scales, fock_prev):
    npeer = lax.axis_size("grid")
    per_dev, npair = owners.shape
    listed_tiles = collocation.shape[2] // dens_tiles.shape[1]
    tile_width = dens_tiles.shape[1]
    stored = dens_tiles.shape[0]
    capacity = max(2, (per_dev * npair + npeer - 1) // npeer)
    flat_owner = owners.reshape(-1)
    flat_slot = slots.reshape(-1)
    peer_ids = jnp.arange(npeer, dtype=jnp.int32)
    onehot = (flat_owner[:, None] == peer_ids[None, :]).astype(jnp.int32)
    running = jnp.cumsum(onehot, axis=0)
    rank = jnp.sum(running * onehot, axis=1) - 1
    requests = jnp.zeros((npeer, capacity), jnp.int32).at[flat_owner, rank].set(flat_slot)
    asked = lax.all_to_all(requests, "grid", split_axis=0, concat_axis=0, tiled=True)
    tiles = dens_tiles[asked].astype(jnp.float32) * dens_scales[asked][:, :, None, None]
    sent = lax.all_to_all(
        tiles.astype(jnp.bfloat16), "grid", split_axis=0, concat_axis=0, tiled=True
    )
    fetched, asked = (sent, asked)
    blocks = fetched[flat_owner, rank].reshape(per_dev, npair, tile_width, tile_width)
    live = jnp.arange(listed_tiles, dtype=jnp.int32)[None, :] < counts[:, None]
    live_pair = (live[:, :, None] & live[:, None, :]).reshape(per_dev, npair)
    blocks = jnp.where(live_pair[:, :, None, None], blocks, jnp.zeros_like(blocks))
    dmats = blocks.reshape(per_dev, listed_tiles, listed_tiles, tile_width, tile_width).transpose(
        0, 1, 3, 2, 4
    )
    dmats = dmats.reshape(per_dev, listed_tiles * tile_width, listed_tiles * tile_width)
    kparts = lax.map(
        lambda items: exchange_contribution(
            items[0], items[1], point_kernel(items[2], items[3]), tile_width, listed_tiles
        ),
        (collocation, dmats, coords, weights),
    )
    kparts = jnp.where(live_pair[:, :, None, None], kparts, 0.0).reshape(
        per_dev * npair, tile_width, tile_width
    )
    outgoing = (
        jnp.zeros((npeer, capacity, tile_width, tile_width), jnp.float32)
        .at[flat_owner, rank]
        .set(kparts)
    )
    received = lax.all_to_all(
        outgoing.astype(jnp.bfloat16), "grid", split_axis=0, concat_axis=0, tiled=True
    ).astype(outgoing.dtype)
    summed = (
        jnp.zeros((stored, tile_width, tile_width), jnp.float32)
        .at[asked.reshape(-1)]
        .add(received.reshape(npeer * capacity, tile_width, tile_width))
    )
    return fock_prev.astype(jnp.float32) - 0.5 * summed


def solution(mesh):
    return jax.shard_map(
        shards,
        mesh=mesh,
        in_specs=(
            P(("groups", "grid"), None, None),
            P(("groups", "grid"), None, None),
            P(("groups", "grid"), None),
            P(("groups", "grid"), None),
            P(("groups", "grid"), None),
            P(("groups", "grid")),
            P(("groups", "grid"), None, None),
            P(("groups", "grid")),
            P(("groups", "grid"), None, None),
        ),
        out_specs=P(("groups", "grid"), None, None),
        check_vma=False,
    )
```

profile of v0, /device:TPU:0, one launch (start us, length us, event | category | flops | bytes accessed | tf_op | source)
XLA Modules:
  0.0 706.7 jit_solution(1214945596496879233)
XLA Ops:
  4.2 11.3 %scatter_fusion = s32[32,8]{0,1:T(8,128)S(1)} fusion(s32[32,8]{0,1:T(8,128)S(1)} %broadcast.133, s32[256]{0:T(256)S(1)} %bitcast.92, s32[256]{0:T(256)S(1)} %reshape.249), kind=kCustom, calls=%fused_computation.3 | custom fusion | bytes 5120 | tf_op jit(solution)/shard_map/scatter | solution.py:49
  15.6 14.2 %all_to_all.22 = s32[32,1,8]{2,1,0:T(1,128)S(1)} all-to-all(s32[32,1,8]{2,1,0:T(1,128)S(1)} %copy.34), channel_id=1, replica_groups=mesh['groups'=1,'grid'=32] {'grid'}, dimensions={0} | all-to-all | bytes 2048 | tf_op jit(solution)/shard_map/all_to_all | solution.py:50
  29.9 8.6 %gather_fusion = bf16[256,128,128]{2,1,0:T(8,128)(2,1)} fusion(bf16[32,128,128]{2,1,0:T(8,128)(2,1)S(1)} %copy-done, s32[1024]{0:T(1024)S(1)} %pad_clamp_fusion), kind=kCustom, calls=%fused_computation | custom fusion | bytes 16778240 | tf_op jit(solution)/shard_map/gather | solution.py:51
  40.5 8.3 %fusion.12 = bf16[32,8,128,128]{3,2,1,0:T(8,128)(2,1)} fusion(bf16[32,8,128,128]{3,2,1,0:T(8,128)(2,1)} %bitcast.96, f32[32,8]{1,0:T(8,128)S(1)} %reshape.234), kind=kLoop, calls=%fused_computation.24 | loop fusion | flops 12582912 | bytes 16778240 | tf_op jit(solution)/shard_map/convert_element_type | solution.py:53
  48.8 4.0 all-to-all-start.1
  53.1 185.9 %all-to-all-done.1 = bf16[32,8,128,128]{3,2,1,0:T(8,128)(2,1)} async-done(((bf16[32,8,128,128]{3,2,1,0:T(8,128)(2,1)}), bf16[32,8,128,128]{3,2,1,0:T(8,128)(2,1)}, u32[]{:S(2)}, u32[]{:S(2)}) %all-to-all-start.1) | async-done | bytes 8388640 | tf_op jit(solution)/shard_map/all_to_all | solution.py:52
  238.9 13.4 %gather_fusion.2 = bf16[256,128,128]{2,1,0:T(8,128)(2,1)} fusion(bf16[32,8,128,128]{3,2,1,0:T(8,128)(2,1)} %all-to-all-done.1, s32[256]{0:T(256)S(1)} %bitcast.98), kind=kCustom, calls=%fused_computation.2 | custom fusion | bytes 16779264 | tf_op jit(solution)/shard_map/gather | solution.py:56
  252.3 7.3 %select_bitcast_fusion = bf16[16,4,128,4,128]{4,2,3,1,0:T(8,128)(2,1)} fusion(bf16[16,4,4,128,128]{4,3,2,1,0:T(8,128)(2,1)} %bitcast.97, pred[16,4,4]{2,1,0:T(4,128)(4,1)S(1)} %copy.36), kind=kLoop, calls=%fused_computation.26 | loop fusion | flops 4194304 | bytes 16777472 | tf_op jit(solution)/shard_map/transpose | solution.py:60
  259.6 11.0 %copy.37 = bf16[16,4,128,4,128]{4,3,2,1,0:T(4,128)(2,1)} copy(bf16[16,4,128,4,128]{4,2,3,1,0:T(8,128)(2,1)} %select_bitcast_fusion) | data formatting | bytes 16777216 | tf_op jit(solution)/shard_map/transpose | solution.py:60
  270.6 13.1 %reshape.219 = bf16[16,512,512]{2,1,0:T(8,128)(2,1)} reshape(bf16[16,4,128,4,128]{4,3,2,1,0:T(4,128)(2,1)} %copy.37) | data formatting | bytes 16777216 | tf_op jit(solution)/shard_map/reshape | solution.py:63
  283.7 109.4 %while.11 = (s32[]{:T(128)}, f32[16,16,128,128]{3,2,1,0:T(8,128)}, bf16[16,512,512]{2,1,0:T(8,128)(2,1)}, bf16[16,512,512]{2,1,0:T(8,128)(2,1)}, f32[16,512]{1,0:T(8,128)}, /*index=5*/f32[16,3,512]{2,0,1:T(8,128)}) while((s32[]{:T(128)}, f32[16,16,128,128]{3,2,1,0:T(8,128)}, bf16[16,512,512]{2,1,0:T(8,128)(2,1)}, ...), condition=%wide.region_6.7_spmd.clone, body=%wide.region_4.6_spmd.sunk.clone | while | flops 808976384 | bytes 10002001 | solution.py:64
  340.3 2.0 convolution_convert_fusion.4
  347.2 2.0 convolution_convert_fusion.4
  354.0 2.0 convolution_convert_fusion.4
  381.4 2.0 convolution_convert_fusion.4
  393.1 11.4 %broadcast_select_fusion = f32[16,16,128,128]{3,2,1,0:T(8,128)} fusion(f32[16,16,128,128]{3,2,1,0:T(8,128)} %get-tuple-element.37, pred[16,16]{1,0:T(8,128)(4,1)S(1)} %copy.35), kind=kLoop, calls=%fused_computation.27 | loop fusion | flops 4194304 | bytes 33554688 | tf_op jit(solution)/shard_map/jit(_where)/select_n | solution.py:70
  404.5 7.8 %broadcast_in_dim.26 = f32[32,8,128,128]{3,2,1,0:T(8,128)} broadcast(f32[]{:T(128)} %constant.17.clone.1), dimensions={} | broadcast | bytes 16777220 | tf_op jit(solution)/shard_map/broadcast_in_dim | solution.py:74
  412.4 47.6 %scatter_fusion.1 = f32[32,8,128,128]{3,2,1,0:T(8,128)} fusion(f32[32,8,128,128]{3,2,1,0:T(8,128)} %broadcast_in_dim.26, s32[256]{0:T(256)S(1)} %bitcast.93, f32[256,128,128]{2,1,0:T(8,128)} %bitcast.94), kind=kCustom, calls=%fused_computation.4 | custom fusion | bytes 50333696 | tf_op jit(solution)/shard_map/scatter | solution.py:76
  460.0 9.2 %convert_element_type.32 = bf16[32,8,128,128]{3,2,1,0:T(8,128)(2,1)} convert(f32[32,8,128,128]{3,2,1,0:T(8,128)} %scatter_fusion.1) | non-fusion elementwise | flops 4194304 | bytes 25165824 | tf_op jit(solution)/shard_map/convert_element_type | solution.py:79
  469.2 3.9 all-to-all-start.2
  474.4 184.8 %all-to-all-done.2 = bf16[32,8,128,128]{3,2,1,0:T(8,128)(2,1)} async-done(((bf16[32,8,128,128]{3,2,1,0:T(8,128)(2,1)}), bf16[32,8,128,128]{3,2,1,0:T(8,128)(2,1)}, u32[]{:S(2)}, u32[]{:S(2)}) %all-to-all-start.2) | async-done | bytes 8388640 | tf_op jit(solution)/shard_map/all_to_all | solution.py:78
  659.2 11.2 %bitcast_convert_fusion = f32[256,128,128]{2,1,0:T(8,128)} fusion(bf16[32,8,128,128]{3,2,1,0:T(8,128)(2,1)} %all-to-all-done.2), kind=kLoop, calls=%fused_computation.25 | loop fusion | flops 4194304 | bytes 25165824 | tf_op jit(solution)/shard_map/reshape | solution.py:84
  670.6 33.2 %scatter_fusion.2 = f32[32,128,128]{2,1,0:T(8,128)S(1)} fusion(f32[32,128,128]{2,1,0:T(8,128)S(1)} %broadcast_in_dim.25, s32[256]{0:T(256)S(1)} %bitcast.104, f32[256,128,128]{2,1,0:T(8,128)} %bitcast_convert_fusion), kind=kCustom, calls=%fused_computation.5 | custom fusion | flops 4194304 | bytes 50332672 | tf_op jit(solution)/shard_map/scatter-add | solution.py:84
  703.8 2.8 multiply_subtract_fusion
  (177 shorter events, 108.7 us)
Async XLA Ops:
  0.0 29.9 %copy-start = (bf16[32,128,128]{2,1,0:T(8,128)(2,1)S(1)}, bf16[32,128,128]{2,1,0:T(8,128)(2,1)}, u32[]{:S(2)}) copy-start(bf16[32,128,128]{2,1,0:T(8,128)(2,1)} %param.17) | copy-start | bytes 3145732
  29.9 8.6 %copy-start.2 = (f32[32]{0:T(128)S(1)}, f32[32]{0:T(128)}, u32[]{:S(2)}) copy-start(f32[32]{0:T(128)} %param.18) | copy-start | bytes 388
  48.8 4.0 copy-start.3
  48.8 190.1 %all-to-all-start.1 = ((bf16[32,8,128,128]{3,2,1,0:T(8,128)(2,1)}), bf16[32,8,128,128]{3,2,1,0:T(8,128)(2,1)}, u32[]{:S(2)}, u32[]{:S(2)}) async-start(bf16[32,8,128,128]{3,2,1,0:T(8,128)(2,1)} %fusion.12), calls=%async_computation.1 | async-start | bytes 16777216 | tf_op jit(solution)/shard_map/all_to_all | solution.py:52
  469.2 190.0 %all-to-all-start.2 = ((bf16[32,8,128,128]{3,2,1,0:T(8,128)(2,1)}), bf16[32,8,128,128]{3,2,1,0:T(8,128)(2,1)}, u32[]{:S(2)}, u32[]{:S(2)}) async-start(bf16[32,8,128,128]{3,2,1,0:T(8,128)(2,1)} %convert_element_type.32), calls=%async_computation.2 | async-start | bytes 16777216 | tf_op jit(solution)/shard_map/all_to_all | solution.py:78
  670.6 36.0 %copy-start.1 = (bf16[32,128,128]{2,1,0:T(8,128)(2,1)S(1)}, bf16[32,128,128]{2,1,0:T(8,128)(2,1)}, u32[]{:S(2)}) copy-start(bf16[32,128,128]{2,1,0:T(8,128)(2,1)} %param.17) | copy-start | bytes 3145732
where the time goes:
time: 712 us; the launch traced here: 707 us
  waiting for transfers between devices  371 us (52%)
  local copies, waits for them, and re-layouts  183 us (26%)
  other arithmetic  90.6 us (13%)
  matrix products  40.1 us (6%)
  blocking collectives  14.2 us (2%)
  starting transfers between devices  7.89 us (1%)
    all_to_all x1, waiting for transfers between devices, shards(): lax.all_to_all(tiles.astype(jnp.bfloat16), 'grid', split_axis=0, concat_a...  186 us
    all_to_all x1, waiting for transfers between devices, shards(): lax.all_to_all(outgoing.astype(jnp.bfloat16), 'grid', split_axis=0, conca...  185 us
    scatter x1, local copies, waits for them, and re-layouts, shards(): outgoing = jnp.zeros((npeer, capacity, tile_width, tile_width), jnp.float...  47.6 us
    dynamic_slice x80, local copies, waits for them, and re-layouts, shards(): lax.map(lambda items: exchange_contribution(items[0], items[1], point_ker...  45.3 us
    scatter-add x1, other arithmetic, shards(): summed = jnp.zeros((stored, tile_width, tile_width), jnp.float32).at[aske...  33.2 us
    dot_general x16, matrix products, exchange_contribution(): jnp.dot(exchange_kernel, projected_field, preferred_element_type=jnp.floa...  32.7 us
    dynamic_update_slice x16, local copies, waits for them, and re-layouts, shards(): lax.map(lambda items: exchange_contribution(items[0], items[1], point_ker...  17.6 us
    all_to_all x1, blocking collectives, shards(): lax.all_to_all(requests, 'grid', split_axis=0, concat_axis=0, tiled=True)  14.2 us
  transfers between devices with their start and end apart: 2, of which 2 were waited for; matrix products, arithmetic and copies ran while one was open for 0% of the time, Pallas kernels for 0%

commit v1 on v0

v1 whole, which is shorter than its diff:
```python
import functools

import jax
import jax.numpy as jnp
from jax import lax
from jax.experimental import pallas as pl
from jax.experimental.pallas import tpu as pltpu
from jax.sharding import PartitionSpec as P

SOFTEN = 0.5
VMEM_BYTES = 48 * 2**20


def metric_kernel(colloc_ref, coords_ref, weights_ref, metric_ref):
    points = colloc_ref.shape[0]
    xyz = coords_ref[...]
    w = weights_ref[...]
    rows = jnp.concatenate([xyz, w, jnp.zeros((4, points), jnp.float32)], axis=0)
    cols = rows.T
    a = colloc_ref[...]
    total = jnp.full((points, points), SOFTEN * SOFTEN, jnp.float32)
    for axis in range(3):
        diff = cols[:, axis : axis + 1] - xyz[axis : axis + 1, :]
        total = total + diff * diff
    kern = (cols[:, 3:4] * w * lax.rsqrt(total)).astype(jnp.bfloat16)
    smeared = jnp.dot(kern, a, preferred_element_type=jnp.float32).astype(jnp.bfloat16)
    metric_ref[...] = lax.dot_general(
        a, smeared, (((0,), (0,)), ((), ())), preferred_element_type=jnp.float32
    ).astype(jnp.bfloat16)


def metric_of(collocation, coords, weights):
    per_dev, points, funcs = collocation.shape
    return pl.pallas_call(
        metric_kernel,
        grid=(per_dev,),
        out_shape=jax.ShapeDtypeStruct((per_dev, funcs, funcs), jnp.bfloat16),
        in_specs=[
            pl.BlockSpec((None, points, funcs), lambda b: (b, 0, 0)),
            pl.BlockSpec((None, 3, points), lambda b: (b, 0, 0)),
            pl.BlockSpec((None, 1, points), lambda b: (b, 0, 0)),
        ],
        out_specs=pl.BlockSpec((None, funcs, funcs), lambda b: (b, 0, 0)),
        compiler_params=pltpu.CompilerParams(vmem_limit_bytes=VMEM_BYTES),
        cost_estimate=pl.CostEstimate(
            flops=4 * per_dev * points * points * funcs,
            bytes_accessed=4 * per_dev * points * funcs,
            transcendentals=per_dev * points * points,
        ),
        name="metric",
    )(collocation, coords, weights[:, None, :])


def pick_kernel(asked_ref, scales_ref, dens_ref, out_ref, scaled):
    stored = dens_ref.shape[0]
    count = out_ref.shape[0]
    step = pl.program_id(0)

    @pl.when(step == 0)
    def _():
        def one(t, carry):
            scaled[t] = (dens_ref[t].astype(jnp.float32) * scales_ref[t]).astype(jnp.bfloat16)
            return carry

        lax.fori_loop(0, stored, one, 0)

    for k in range(count):
        out_ref[k] = scaled[asked_ref[step * count + k]]


def pick(asked, scales, dens, chunk):
    total = asked.shape[0]
    stored, width, _ = dens.shape
    return pl.pallas_call(
        pick_kernel,
        out_shape=jax.ShapeDtypeStruct((total, width, width), jnp.bfloat16),
        grid_spec=pltpu.PrefetchScalarGridSpec(
            num_scalar_prefetch=2,
            grid=(total // chunk,),
            in_specs=[pl.BlockSpec((stored, width, width), lambda s, *_: (0, 0, 0))],
            out_specs=pl.BlockSpec((chunk, width, width), lambda s, *_: (s, 0, 0)),
            scratch_shapes=[pltpu.VMEM((stored, width, width), jnp.bfloat16)],
        ),
        compiler_params=pltpu.CompilerParams(vmem_limit_bytes=VMEM_BYTES),
        name="pick",
    )(asked, scales, dens)


def apply_kernel(listed, pos_ref, counts_ref, fetched_ref, metric_ref, out_ref, dmat):
    width = fetched_ref.shape[1]
    b = pl.program_id(0)
    count = counts_ref[b]
    for i in range(listed):
        for j in range(listed):
            live = max(i, j) < count
            where = pos_ref[b * listed * listed + i * listed + j]
            tile = fetched_ref[where]
            dmat[i * width : (i + 1) * width, j * width : (j + 1) * width] = jnp.where(
                live, tile, jnp.zeros_like(tile)
            )
    parts = jnp.dot(metric_ref[...], dmat[...], preferred_element_type=jnp.float32)
    for i in range(listed):
        for j in range(listed):
            live = max(i, j) < count
            where = pos_ref[b * listed * listed + i * listed + j]
            part = parts[i * width : (i + 1) * width, j * width : (j + 1) * width]
            part = part.astype(jnp.bfloat16)
            out_ref[where] = jnp.where(live, part, jnp.zeros_like(part))


def apply_metric(pos, counts, fetched, metric):
    total, width, _ = fetched.shape
    per_dev, funcs, _ = metric.shape
    return pl.pallas_call(
        functools.partial(apply_kernel, funcs // width),
        out_shape=jax.ShapeDtypeStruct((total, width, width), jnp.bfloat16),
        grid_spec=pltpu.PrefetchScalarGridSpec(
            num_scalar_prefetch=2,
            grid=(per_dev,),
            in_specs=[
                pl.BlockSpec(
                    (total, width, width), lambda b, *_: (0, 0, 0), pipeline_mode=pl.Buffered(1)
                ),
                pl.BlockSpec((None, funcs, funcs), lambda b, *_: (b, 0, 0)),
            ],
            out_specs=pl.BlockSpec((total, width, width), lambda b, *_: (0, 0, 0)),
            scratch_shapes=[pltpu.VMEM((funcs, funcs), jnp.bfloat16)],
        ),
        compiler_params=pltpu.CompilerParams(vmem_limit_bytes=VMEM_BYTES),
        name="apply_metric",
    )(pos, counts, fetched, metric)


def update_kernel(asked_ref, received_ref, prev_ref, out_ref):
    count = received_ref.shape[0]
    step = pl.program_id(0)

    @pl.when(step == 0)
    def _():
        out_ref[...] = prev_ref[...].astype(jnp.float32)

    for k in range(count):
        slot = asked_ref[step * count + k]
        out_ref[slot] = out_ref[slot] - 0.5 * received_ref[k].astype(jnp.float32)


def update(asked, received, prev, chunk):
    total, width, _ = received.shape
    stored = prev.shape[0]
    return pl.pallas_call(
        update_kernel,
        out_shape=jax.ShapeDtypeStruct((stored, width, width), jnp.float32),
        grid_spec=pltpu.PrefetchScalarGridSpec(
            num_scalar_prefetch=1,
            grid=(total // chunk,),
            in_specs=[
                pl.BlockSpec((chunk, width, width), lambda s, *_: (s, 0, 0)),
                pl.BlockSpec((stored, width, width), lambda s, *_: (0, 0, 0)),
            ],
            out_specs=pl.BlockSpec((stored, width, width), lambda s, *_: (0, 0, 0)),
        ),
        compiler_params=pltpu.CompilerParams(vmem_limit_bytes=VMEM_BYTES),
        name="update",
    )(asked, received, prev)


def shards(collocation, coords, weights, owners, slots, counts, dens_tiles, dens_scales, fock_prev):
    npeer = lax.axis_size("grid")
    per_dev, npair = owners.shape
    width = dens_tiles.shape[1]
    entries = per_dev * npair
    capacity = entries // npeer
    flat_owner = owners.reshape(-1)
    flat_slot = slots.reshape(-1)
    onehot = (flat_owner[:, None] == jnp.arange(npeer, dtype=jnp.int32)[None, :]).astype(jnp.bfloat16)
    before = jnp.tril(jnp.ones((entries, entries), jnp.bfloat16), -1)
    running = jnp.dot(before, onehot, preferred_element_type=jnp.float32)
    rank = jnp.sum(running * onehot.astype(jnp.float32), axis=1).astype(jnp.int32)
    pos = flat_owner * capacity + rank
    ranked = jnp.where(
        rank[:, None] == jnp.arange(capacity, dtype=jnp.int32)[None, :], flat_slot[:, None], 0
    )
    requests = jnp.dot(
        onehot.T, ranked.astype(jnp.bfloat16), preferred_element_type=jnp.float32
    ).astype(jnp.int32)
    asked = lax.all_to_all(requests, "grid", split_axis=0, concat_axis=0, tiled=True).reshape(-1)
    chunk = 16
    tiles = pick(asked, dens_scales, dens_tiles, chunk)
    metric = metric_of(collocation, coords, weights)
    fetched = lax.all_to_all(
        tiles.reshape(npeer, capacity, width, width), "grid", split_axis=0, concat_axis=0, tiled=True
    ).reshape(entries, width, width)
    outgoing = apply_metric(pos, counts, fetched, metric)
    received = lax.all_to_all(
        outgoing.reshape(npeer, capacity, width, width), "grid", split_axis=0, concat_axis=0, tiled=True
    ).reshape(entries, width, width)
    return update(asked, received, fock_prev, chunk)


def solution(mesh):
    split = ("groups", "grid")
    return jax.shard_map(
        shards,
        mesh=mesh,
        in_specs=(
            P(split, None, None),
            P(split, None, None),
            P(split, None),
            P(split, None),
            P(split, None),
            P(split),
            P(split, None, None),
            P(split),
            P(split, None, None),
        ),
        out_specs=P(split, None, None),
        check_vma=False,
    )
```

time: 712 us -> 437 us (0.61)
  waiting for transfers between devices: 371 us -> 163 us
  blocking collectives: 14.2 us -> 202 us
  local copies, waits for them, and re-layouts: 183 us -> 4.22 us
  other arithmetic: 90.6 us -> 0.7 us
  Pallas kernels: 0 us -> 62.9 us
  matrix products: 40.1 us -> 0.56 us
    all_to_all x2 -> x1, waiting for transfers between devices: 371 us -> 163 us  [shards(): lax.all_to_all(tiles.reshape(npeer, capacity, width, width), 'grid', spli...]
    all_to_all x0 -> x1, blocking collectives: none -> 187 us  [shards(): lax.all_to_all(outgoing.reshape(npeer, capacity, width, width), 'grid', s...]
    pallas_call x0 -> x4, Pallas kernels: none -> 62.9 us  [the longest x1 23.4 us: metric_of(): pl.pallas_call(metric_kernel, grid=(per_dev,), out_shape=jax.ShapeDtypeSt...]
    scatter x2 -> x0, local copies, waits for them, and re-layouts: 59 us -> none  [the longest x1 47.6 us: shards(): outgoing = jnp.zeros((npeer, capacity, tile_width, tile_width), jnp.float...]
    dynamic_slice x80 -> x0, local copies, waits for them, and re-layouts: 45.3 us -> none  [shards(): lax.map(lambda items: exchange_contribution(items[0], items[1], point_ker...]
    dot_general x32 -> x2, matrix products: 40.1 us -> 0.56 us  [the longest x1 0.29 us: shards(): jnp.dot(onehot.T, ranked.astype(jnp.bfloat16), preferred_element_type=jnp...]
    scatter-add x1 -> x0, other arithmetic: 33.2 us -> none  [shards(): summed = jnp.zeros((stored, tile_width, tile_width), jnp.float32).at[aske...]
    gather x4 -> x0, local copies, waits for them, and re-layouts: 24 us -> none  [the longest x1 13.4 us: shards(): fetched[flat_owner, rank].reshape(per_dev, npair, tile_width, tile_width)]
  transfers between devices with their start and end apart: 2 -> 1, of which waited for: 2 -> 1; matrix products, arithmetic and copies ran while one was open for 0% -> 0% of each run, Pallas kernels for 0% -> 5%
where the time goes in v1:
time: 437 us; the launch traced here: 436 us
  blocking collectives  202 us (46%)
  waiting for transfers between devices  163 us (37%)
  Pallas kernels  62.9 us (14%)
    all_to_all x1, blocking collectives, shards(): lax.all_to_all(outgoing.reshape(npeer, capacity, width, width), 'grid', s...  187 us
    all_to_all x1, waiting for transfers between devices, shards(): lax.all_to_all(tiles.reshape(npeer, capacity, width, width), 'grid', spli...  163 us
    pallas_call x1, Pallas kernels, metric_of(): pl.pallas_call(metric_kernel, grid=(per_dev,), out_shape=jax.ShapeDtypeSt...  23.4 us
    pallas_call x1, Pallas kernels, apply_metric(): pl.pallas_call(functools.partial(apply_kernel, funcs // width), out_shape...  19.7 us
    all_to_all x1, blocking collectives, shards(): lax.all_to_all(requests, 'grid', split_axis=0, concat_axis=0, tiled=True)  14.2 us
    pallas_call x1, Pallas kernels, update(): pl.pallas_call(update_kernel, out_shape=jax.ShapeDtypeStruct((stored, wid...  11.9 us
  transfers between devices with their start and end apart: 1, of which 1 were waited for; matrix products, arithmetic and copies ran while one was open for 0% of the time, Pallas kernels for 5%

profile of v1, /device:TPU:0, one launch (start us, length us, event | category | flops | bytes accessed | tf_op | source)
XLA Modules:
  0.0 436.4 jit_solution(7879075343830934209)
XLA Ops:
  0.0 0.8 eq.28
  0.8 0.3 fusion
  1.1 0.8 broadcast_in_dim.29
  1.8 0.3 fusion.1
  2.1 0.1 copy.13
  2.2 14.2 %all_to_all.19 = s32[32,1,8]{2,1,0:T(1,128)S(1)} all-to-all(s32[32,1,8]{2,1,0:T(1,128)S(1)} %copy.13), channel_id=1, replica_groups=mesh['groups'=1,'grid'=32] {'grid'}, dimensions={0} | all-to-all | bytes 2048 | tf_op jit(solution)/shard_map/all_to_all | solution.py:186
  16.5 0.5 broadcast.6
  17.0 0.7 reduce.3
  17.7 0.1 reshape.24.asked_ref
  17.8 0.0 copy-start
  17.8 1.2 copy-done
  19.0 0.7 copy-done.2
  19.6 7.8 %pick.1 = bf16[256,128,128]{2,1,0:T(8,128)(2,1)} custom-call(s32[256]{0:T(256)S(1)} %reshape.24.asked_ref, f32[32]{0:T(128)S(1)} %copy-done.2, bf16[32,128,128]{2,1,0:T(8,128)(2,1)S(1)} %copy-done), custom_call_target="tpu_custom_call" | custom-call | tf_op jit(solution)/shard_map/pick/pallas_call | solution.py:74
  27.5 3.8 all-to-all-start.1
  31.3 0.0 copy-done.4
  31.3 0.1 copy.14.coords_ref
  31.4 0.0 copy-done.5
  31.4 0.0 copy-start.3
  31.4 23.4 %metric.1.metric_ref = bf16[16,512,512]{2,1,0:T(8,128)(2,1)} custom-call(bf16[16,512,512]{2,1,0:T(8,128)(2,1)} %colloc_ref.1, f32[16,3,512]{2,1,0:T(4,128)S(1)} %copy.14.coords_ref, f32[16,1,512]{2,1,0:T(1,128)S(1)} %broadcast_in_dim.32.weights_ref), custom_call_target="tpu_custom_call" | custom-call | flops 8589934592 | bytes 16777216 | tf_op jit(solution)/shard_map/metric/pallas_call | solution.py:34
  54.8 162.6 %all-to-all-done.1 = bf16[32,8,128,128]{3,2,1,0:T(8,128)(2,1)} async-done(((bf16[32,8,128,128]{3,2,1,0:T(8,128)(2,1)}), bf16[32,8,128,128]{3,2,1,0:T(8,128)(2,1)}, u32[]{:S(2)}, u32[]{:S(2)}) %all-to-all-start.1) | async-done | bytes 8388640 | tf_op jit(solution)/shard_map/all_to_all | solution.py:190
  217.4 0.0 copy-done.3
  217.4 19.7 %apply_metric.1 = bf16[256,128,128]{2,1,0:T(8,128)(2,1)} custom-call(s32[256]{0:T(256)S(1)} %multiply_add_fusion.pos_ref, s32[16]{0:T(128)S(1)} %copy-done.3, bf16[256,128,128]{2,1,0:T(8,128)(2,1)} %bitcast.2.fetched_ref, bf16[16,512,512]{2,1,0:T(8,128)(2,1)} %metric.1.metric_ref), custom_call_target="tpu_custom_call" | custom-call | tf_op jit(solution)/shard_map/apply_metric/pallas_call | solution.py:114
  237.1 187.3 %all_to_all.20 = bf16[32,8,128,128]{3,2,1,0:T(8,128)(2,1)} all-to-all(bf16[32,8,128,128]{3,2,1,0:T(8,128)(2,1)} %bitcast.8), channel_id=1, replica_groups=mesh['groups'=1,'grid'=32] {'grid'}, dimensions={0} | all-to-all | bytes 16777216 | tf_op jit(solution)/shard_map/all_to_all | solution.py:194
  424.4 11.9 %update.1 = f32[32,128,128]{2,1,0:T(8,128)} custom-call(s32[256]{0:T(256)S(1)} %reshape.24.asked_ref, bf16[256,128,128]{2,1,0:T(8,128)(2,1)} %bitcast.7, bf16[32,128,128]{2,1,0:T(8,128)(2,1)S(1)} %copy-done.1), custom_call_target="tpu_custom_call" | custom-call | tf_op jit(solution)/shard_map/update/pallas_call | solution.py:150
  (9 shorter events, 0.0 us)
Async XLA Ops:
  17.8 1.2 copy-start
  19.0 0.7 copy-start.2
  27.5 3.8 copy-start.4
  27.5 3.9 copy-start.5
  27.5 190.0 %all-to-all-start.1 = ((bf16[32,8,128,128]{3,2,1,0:T(8,128)(2,1)}), bf16[32,8,128,128]{3,2,1,0:T(8,128)(2,1)}, u32[]{:S(2)}, u32[]{:S(2)}) async-start(bf16[32,8,128,128]{3,2,1,0:T(8,128)(2,1)} %bitcast.6), calls=%async_computation.1 | async-start | bytes 16777216 | tf_op jit(solution)/shard_map/all_to_all | solution.py:190
  31.4 186.0 %copy-start.3 = (s32[16]{0:T(128)S(1)}, s32[16]{0:T(128)}, u32[]{:S(2)}) copy-start(s32[16]{0:T(128)} %counts_ref.1) | copy-start | bytes 196
  237.1 187.3 %copy-start.1 = (bf16[32,128,128]{2,1,0:T(8,128)(2,1)S(1)}, bf16[32,128,128]{2,1,0:T(8,128)(2,1)}, u32[]{:S(2)}) copy-start(bf16[32,128,128]{2,1,0:T(8,128)(2,1)} %prev_ref.1) | copy-start | bytes 3145732

commit v2 on v1

--- a/solution.py
+++ b/solution.py
@@ -164,6 +164,349 @@
     )(asked, received, prev)
 
 
+def mate(z, lane, plane):
+    return {"grid": z * plane + lane}
+
+
+def greet(z, q, plane, line):
+    barrier = pltpu.get_barrier_semaphore()
+    for k in range(1, plane):
+        pl.semaphore_signal(
+            barrier, inc=1, device_id=mate(z, lax.rem(q + k, plane), plane), device_id_type=pl.DeviceIdType.MESH
+        )
+
+    @pl.when(z > 0)
+    def _():
+        pl.semaphore_signal(barrier, inc=1, device_id=mate(z - 1, q, plane), device_id_type=pl.DeviceIdType.MESH)
+
+    @pl.when(z < line - 1)
+    def _():
+        pl.semaphore_signal(barrier, inc=1, device_id=mate(z + 1, q, plane), device_id_type=pl.DeviceIdType.MESH)
+
+    pl.semaphore_wait(barrier, plane - 1 + jnp.where(z > 0, 1, 0) + jnp.where(z < line - 1, 1, 0))
+
+
+def fetch_kernel(
+    plane, line, asked_ref, scales_ref, dens_ref, colloc_ref, coords_ref, weights_ref, fetched_ref, metric_ref,
+    *scratch
+):
+    pools, (stage, hop_send, hop_recv, local_sem, send_sem, recv_sem) = scratch[:line], scratch[line:]
+    capacity = fetched_ref.shape[1]
+    stored = dens_ref.shape[0]
+    batches = colloc_ref.shape[0]
+    me = lax.axis_index("grid")
+    z, q = me // plane, lax.rem(me, plane)
+
+    def scale(t, carry):
+        pools[0][t] = (dens_ref[t].astype(jnp.float32) * scales_ref[t]).astype(jnp.bfloat16)
+        return carry
+
+    lax.fori_loop(0, stored, scale, 0)
+    greet(z, q, plane, line)
+
+    def hop(slot, up):
+        to_slot = (slot + 1 if up else slot - 1) % line
+        return pltpu.make_async_remote_copy(
+            src_ref=pools[slot],
+            dst_ref=pools[to_slot],
+            send_sem=hop_send.at[line if (slot == 0 and not up) else slot],
+            recv_sem=hop_recv.at[to_slot],
+            device_id=mate(z + 1 if up else z - 1, q, plane),
+            device_id_type=pl.DeviceIdType.MESH,
+        )
+
+    def hops(slot, act):
+        if slot + 1 < line:
+
+            @pl.when((z >= slot) & (z < line - 1))
+            def _():
+                act(hop(slot, True))
+
+        if slot != 1:
+
+            @pl.when(((z < slot) | (slot == 0)) & (z > 0))
+            def _():
+                act(hop(slot, False))
+
+    def to_mate(slot, k):
+        owner = lax.rem(z - slot + line, line) * plane + q
+        return pltpu.make_async_remote_copy(
+            src_ref=stage.at[slot, k],
+            dst_ref=fetched_ref.at[owner],
+            send_sem=send_sem.at[slot, k],
+            recv_sem=recv_sem.at[slot, k],
+            device_id=mate(z, lax.rem(q + k, plane), plane),
+            device_id_type=pl.DeviceIdType.MESH,
+        )
+
+    def to_self(slot):
+        owner = lax.rem(z - slot + line, line) * plane + q
+        return pltpu.make_async_copy(stage.at[slot, 0], fetched_ref.at[owner], local_sem.at[slot])
+
+    def serve(slot):
+        if slot:
+            hop(slot - 1, True).wait_recv()
+        hops(slot, lambda copy: copy.start())
+        source = lax.rem(z - slot + line, line)
+
+        def fill(k):
+            base = (lax.rem(q + k, plane) * line + source) * capacity
+            for r in range(capacity):
+                stage[slot, k, r] = pools[slot][asked_ref[base + r]]
+
+        def one(k, carry):
+            fill(k)
+            to_mate(slot, k).start()
+            return carry
+
+        lax.fori_loop(1, plane, one, 0)
+        fill(0)
+        to_self(slot).start()
+
+    def metrics(first, last):
+        def one(b, carry):
+            metric_kernel(colloc_ref.at[b], coords_ref.at[b], weights_ref.at[b], metric_ref.at[b])
+            return carry
+
+        lax.fori_loop(first, last, one, 0)
+
+    serve(0)
+    for d in range(1, line):
+        metrics(batches * (d - 1) // (line - 1), batches * d // (line - 1))
+        if 2 * d == line:
+            serve(d)
+        else:
+            pl.when(z >= d)(functools.partial(serve, d))
+            pl.when(z + d < line)(functools.partial(serve, line - d))
+    for slot in range(line):
+        hops(slot, lambda copy: copy.wait_send())
+        to_self(slot).wait()
+
+        def finish(k, carry):
+            to_mate(slot, k).wait()
+            return carry
+
+        lax.fori_loop(1, plane, finish, 0)
+
+
+def fetch(asked, scales, dens, collocation, coords, weights, plane, line, capacity):
+    stored, width, _ = dens.shape
+    per_dev, points, funcs = collocation.shape
+    vmem, smem = pl.BlockSpec(memory_space=pltpu.VMEM), pl.BlockSpec(memory_space=pltpu.SMEM)
+    return pl.pallas_call(
+        functools.partial(fetch_kernel, plane, line),
+        out_shape=(
+            jax.ShapeDtypeStruct((line * plane, capacity, width, width), jnp.bfloat16),
+            jax.ShapeDtypeStruct((per_dev, funcs, funcs), jnp.bfloat16),
+        ),
+        in_specs=[smem, smem, vmem, vmem, vmem, vmem],
+        out_specs=(pl.BlockSpec(memory_space=pl.ANY), vmem),
+        scratch_shapes=[pltpu.VMEM((stored, width, width), jnp.bfloat16)] * line
+        + [
+            pltpu.VMEM((line, plane, capacity, width, width), jnp.bfloat16),
+            pltpu.SemaphoreType.DMA((line + 1,)),
+            pltpu.SemaphoreType.DMA((line,)),
+            pltpu.SemaphoreType.DMA((line,)),
+            pltpu.SemaphoreType.DMA((line, plane)),
+            pltpu.SemaphoreType.DMA((line, plane)),
+        ],
+        compiler_params=pltpu.CompilerParams(
+            collective_id=0, has_side_effects=True, vmem_limit_bytes=VMEM_BYTES
+        ),
+        name="fetch",
+    )(asked, scales, dens, collocation, coords, weights[:, None, :])
+
+
+def return_kernel(
+    plane, line, perm_ref, same_ref, last_ref, has_ref, outgoing_ref, prev_ref, out_ref, *scratch
+):
+    received, rest = scratch[:line], scratch[line:]
+    running, part, inbox, hop_send, hop_recv, local_sem, send_sem, recv_sem = rest
+    capacity = outgoing_ref.shape[1]
+    stored, width, _ = prev_ref.shape
+    entries = plane * capacity
+    me = lax.axis_index("grid")
+    z, q = me // plane, lax.rem(me, plane)
+    order = [jnp.where(z == 0, line - 1 - p, jnp.where(z == line - 1, (p + 1) % line, (2, 1, 3, 0)[p])) for p in range(line)]
+    greet(z, q, plane, line)
+
+    def to_mate(p, k):
+        to = lax.rem(q + k, plane)
+        return pltpu.make_async_remote_copy(
+            src_ref=outgoing_ref.at[lax.rem(z + order[p], line) * plane + to],
+            dst_ref=received[p].at[pl.ds(q * capacity, capacity)],
+            send_sem=send_sem.at[p, k],
+            recv_sem=recv_sem.at[p, k],
+            device_id=mate(z, to, plane),
+            device_id_type=pl.DeviceIdType.MESH,
+        )
+
+    def to_self(p):
+        return pltpu.make_async_copy(
+            outgoing_ref.at[lax.rem(z + order[p], line) * plane + q],
+            received[p].at[pl.ds(q * capacity, capacity)],
+            local_sem.at[p],
+        )
+
+    def exchange(p):
+        def one(k, carry):
+            to_mate(p, k).start()
+            return carry
+
+        lax.fori_loop(1, plane, one, 0)
+        to_self(p).start()
+
+    def hop(p, up):
+        to = order[p] - 1 if up else order[p] + 1
+        return pltpu.make_async_remote_copy(
+            src_ref=part.at[p],
+            dst_ref=inbox.at[to],
+            send_sem=hop_send.at[p],
+            recv_sem=hop_recv.at[to],
+            device_id=mate(z + 1 if up else z - 1, q, plane),
+            device_id_type=pl.DeviceIdType.MESH,
+        )
+
+    def arrival(slot):
+        return pltpu.make_async_remote_copy(
+            src_ref=part.at[0],
+            dst_ref=inbox.at[slot],
+            send_sem=hop_send.at[0],
+            recv_sem=hop_recv.at[slot],
+            device_id=mate(z, lax.rem(q + 1, plane), plane),
+            device_id_type=pl.DeviceIdType.MESH,
+        )
+
+    def gather(p):
+        def finish(k, carry):
+            to_mate(p, k).wait()
+            return carry
+
+        lax.fori_loop(1, plane, finish, 0)
+        to_self(p).wait()
+        if p + 2 < line:
+            exchange(p + 2)
+        row = lax.rem(z + order[p], line)
+
+        def one(k, total):
+            tile = received[p][perm_ref[row * entries + k]].astype(jnp.float32)
+            total = jnp.where(same_ref[row * entries + k] != 0, total, 0.0) + tile
+            running[k] = total
+            return total
+
+        lax.fori_loop(0, entries, one, jnp.zeros((width, width), jnp.float32))
+
+    def slot_sum(p, t):
+        row = lax.rem(z + order[p], line)
+        return jnp.where(has_ref[row * stored + t] != 0, running[last_ref[row * stored + t]], 0.0)
+
+    def each(body):
+        def one(t, carry):
+            body(t)
+            return carry
+
+        lax.fori_loop(0, stored, one, 0)
+
+    exchange(0)
+    exchange(1)
+    for p in range(line - 1):
+        gather(p)
+        up = z + order[p] < line
+        feeds = jnp.where(up, z > 0, z < line - 1)
+
+        @pl.when(feeds)
+        def _():
+            arrival(order[p]).wait_recv()
+
+            def body(t):
+                part[p, t] = (slot_sum(p, t) + inbox[order[p], t].astype(jnp.float32)).astype(jnp.bfloat16)
+
+            each(body)
+
+        @pl.when(jnp.logical_not(feeds))
+        def _():
+            def body(t):
+                part[p, t] = slot_sum(p, t).astype(jnp.bfloat16)
+
+            each(body)
+
+        pl.when(up)(lambda: hop(p, True).start())
+        pl.when(jnp.logical_not(up))(lambda: hop(p, False).start())
+    gather(line - 1)
+
+    def first(t):
+        out_ref[t] = prev_ref[t].astype(jnp.float32) - 0.5 * slot_sum(line - 1, t)
+
+    each(first)
+    for slot, there in ((0, z > 0), (line, z < line - 1)):
+
+        @pl.when(there)
+        def _():
+            arrival(slot).wait_recv()
+
+            def body(t):
+                out_ref[t] = out_ref[t] - 0.5 * inbox[slot, t].astype(jnp.float32)
+
+            each(body)
+
+    for p in range(line - 1):
+        arrival_of = pltpu.make_async_remote_copy(
+            src_ref=part.at[p],
+            dst_ref=inbox.at[0],
+            send_sem=hop_send.at[p],
+            recv_sem=hop_recv.at[0],
+            device_id=mate(z, lax.rem(q + 1, plane), plane),
+            device_id_type=pl.DeviceIdType.MESH,
+        )
+        arrival_of.wait_send()
+
+
+def give_back(tables, outgoing, prev, plane, line):
+    stored, width, _ = prev.shape
+    capacity = outgoing.shape[1]
+    vmem, smem = pl.BlockSpec(memory_space=pltpu.VMEM), pl.BlockSpec(memory_space=pltpu.SMEM)
+    return pl.pallas_call(
+        functools.partial(return_kernel, plane, line),
+        out_shape=jax.ShapeDtypeStruct((stored, width, width), jnp.float32),
+        in_specs=[smem, smem, smem, smem, pl.BlockSpec(memory_space=pl.ANY), vmem],
+        out_specs=vmem,
+        scratch_shapes=[pltpu.VMEM((plane * capacity, width, width), jnp.bfloat16)] * line
+        + [
+            pltpu.VMEM((plane * capacity, width, width), jnp.float32),
+            pltpu.VMEM((line - 1, stored, width, width), jnp.bfloat16),
+            pltpu.VMEM((line + 1, stored, width, width), jnp.bfloat16),
+            pltpu.SemaphoreType.DMA((line - 1,)),
+            pltpu.SemaphoreType.DMA((line + 1,)),
+            pltpu.SemaphoreType.DMA((line,)),
+            pltpu.SemaphoreType.DMA((line, plane)),
+            pltpu.SemaphoreType.DMA((line, plane)),
+        ],
+        compiler_params=pltpu.CompilerParams(
+            collective_id=1, has_side_effects=True, vmem_limit_bytes=VMEM_BYTES
+        ),
+        name="give_back",
+    )(*tables, outgoing, prev)
+
+
+def slot_tables(asked, stored):
+    entries = asked.shape[1]
+    index = jnp.arange(entries, dtype=jnp.int32)
+    earlier = (asked[:, None, :] < asked[:, :, None]) | (
+        (asked[:, None, :] == asked[:, :, None]) & (index[None, None, :] < index[None, :, None])
+    )
+    place = jnp.sum(earlier.astype(jnp.int32), axis=2)
+    at = place[:, None, :] == index[None, :, None]
+    perm = jnp.sum(jnp.where(at, index[None, None, :], 0), axis=2)
+    shared = jnp.any(
+        (asked[:, None, :] == asked[:, :, None]) & (index[None, None, :] < index[None, :, None]), axis=2
+    )
+    same = jnp.sum((at & shared[:, None, :]).astype(jnp.int32), axis=2)
+    slot = jnp.arange(stored, dtype=jnp.int32)[None, :, None]
+    last = jnp.maximum(jnp.sum((asked[:, None, :] <= slot).astype(jnp.int32), axis=2) - 1, 0)
+    has = jnp.any(asked[:, None, :] == slot, axis=2).astype(jnp.int32)
+    return tuple(table.reshape(-1) for table in (perm, same, last, has))
+
+
 def shards(collocation, coords, weights, owners, slots, counts, dens_tiles, dens_scales, fock_prev):
     npeer = lax.axis_size("grid")
     per_dev, npair = owners.shape
@@ -183,6 +526,20 @@
     requests = jnp.dot(
         onehot.T, ranked.astype(jnp.bfloat16), preferred_element_type=jnp.float32
     ).astype(jnp.int32)
+    plane = 8
+    line = npeer // plane
+    if line == 4:
+        wanted = requests.reshape(line, plane, capacity).transpose(1, 0, 2)
+        groups = [[z * plane + k for k in range(plane)] for z in range(line)]
+        asked = lax.all_to_all(
+            wanted, "grid", split_axis=0, concat_axis=0, tiled=True, axis_index_groups=groups
+        )
+        tables = slot_tables(asked.transpose(1, 0, 2).reshape(line, plane * capacity), dens_tiles.shape[0])
+        fetched, metric = fetch(
+            asked.reshape(-1), dens_scales, dens_tiles, collocation, coords, weights, plane, line, capacity
+        )
+        outgoing = apply_metric(pos, counts, fetched.reshape(entries, width, width), metric)
+        return give_back(tables, outgoing.reshape(npeer, capacity, width, width), fock_prev, plane, line)
     asked = lax.all_to_all(requests, "grid", split_axis=0, concat_axis=0, tiled=True).reshape(-1)
     chunk = 16
     tiles = pick(asked, dens_scales, dens_tiles, chunk)

time: 437 us -> 245 us (0.56)
  blocking collectives: 202 us -> 0 us
  Pallas kernels: 62.9 us -> 226 us
  waiting for transfers between devices: 163 us -> 2.98 us
    all_to_all x2 -> x0, blocking collectives: 202 us -> none  [the longest x1 187 us: shards(): lax.all_to_all(outgoing.reshape(npeer, capacity, width, width), 'grid', s...]
    pallas_call x3 -> x2, Pallas kernels: 43.1 us -> 206 us  [the longest x1 104 us: fetch(): pl.pallas_call(functools.partial(fetch_kernel, plane, line), out_shape=(j...]
    all_to_all x1, waiting for transfers between devices: 163 us -> 2.98 us  [shards(): lax.all_to_all(wanted, 'grid', split_axis=0, concat_axis=0, tiled=True, a...]
  transfers between devices with their start and end apart: 1 -> 1, of which waited for: 1 -> 1; matrix products, arithmetic and copies ran while one was open for 0% -> 1% of each run, Pallas kernels for 5% -> 0%
where the time goes in v2:
time: 245 us; the launch traced here: 244 us
  Pallas kernels  226 us (92%)
  local copies, waits for them, and re-layouts  7.8 us (3%)
  starting transfers between devices  5.17 us (2%)
  waiting for transfers between devices  2.98 us (1%)
    pallas_call x1, Pallas kernels, fetch(): pl.pallas_call(functools.partial(fetch_kernel, plane, line), out_shape=(j...  104 us
    pallas_call x1, Pallas kernels, give_back(): pl.pallas_call(functools.partial(return_kernel, plane, line), out_shape=j...  103 us
    pallas_call x1, Pallas kernels, apply_metric(): pl.pallas_call(functools.partial(apply_kernel, funcs // width), out_shape...  19.7 us
    all_to_all x1, starting transfers between devices, shards(): lax.all_to_all(wanted, 'grid', split_axis=0, concat_axis=0, tiled=True, a...  5.17 us
  transfers between devices with their start and end apart: 1, of which 1 were waited for; matrix products, arithmetic and copies ran while one was open for 1% of the time, Pallas kernels for 0%

profile of v2, /device:TPU:0, one launch (start us, length us, event | category | flops | bytes accessed | tf_op | source)
XLA Modules:
  0.0 243.6 jit_solution(18191901005335153906)
XLA Ops:
  0.0 0.8 eq.24
  0.8 0.8 broadcast_in_dim.50
  1.6 0.3 fusion
  1.9 0.3 convolution_convert_fusion
  2.2 0.7 copy.14
  2.9 5.2 %all-to-all-start = ((s32[8,4,8]{2,1,0:T(4,128)}), s32[8,4,8]{2,1,0:T(4,128)S(1)}, u32[]{:S(2)}, u32[]{:S(2)}) async-start(s32[8,4,8]{2,1,0:T(4,128)} %bitcast), calls=%async_computation | async-start | bytes 32768 | tf_op jit(solution)/shard_map/all_to_all | solution.py:534
  8.1 0.8 broadcast_in_dim.55.weights_ref
  8.9 1.0 copy.16.coords_ref
  9.9 3.0 %all-to-all-done = s32[8,4,8]{2,1,0:T(4,128)S(1)} async-done(((s32[8,4,8]{2,1,0:T(4,128)}), s32[8,4,8]{2,1,0:T(4,128)S(1)}, u32[]{:S(2)}, u32[]{:S(2)}) %all-to-all-start) | async-done | bytes 1056 | tf_op jit(solution)/shard_map/all_to_all | solution.py:534
  12.8 0.1 lt.19
  12.9 0.1 fusion.11
  13.1 0.2 fusion.5
  13.3 0.2 convert_reduce_fusion.1
  13.6 0.1 convert_reduce_fusion.2
  13.7 0.1 max.12.last_ref
  13.8 0.1 reshape.59.has_ref
  13.9 0.2 convert_reduce_fusion
  14.3 0.1 reshape.56.asked_ref
  14.4 1.2 copy-done
  15.6 0.7 copy-done.2
  16.3 103.5 %fetch.1 = (bf16[32,8,128,128]{3,2,1,0:T(8,128)(2,1)}, bf16[16,512,512]{2,1,0:T(8,128)(2,1)}) custom-call(s32[256]{0:T(256)S(1)} %reshape.56.asked_ref, f32[32]{0:T(128)S(1)} %copy-done.2, bf16[32,128,128]{2,1,0:T(8,128)(2,1)S(1)} %copy-done, bf16[16,512,512]{2,1,0:T(8,128)(2,1)} %colloc_ref.1, f32[16,3,512]{2,1,0:T(4,128)S(1)} %copy.16.coords_ref, ...), custom_call_target="tpu_custom_call" | custom-call | tf_op jit(solution)/shard_map/fetch/pallas_call | solution.py:296
  119.8 19.7 %apply_metric.1 = bf16[256,128,128]{2,1,0:T(8,128)(2,1)} custom-call(s32[256]{0:T(256)S(1)} %multiply_add_fusion.pos_ref, s32[16]{0:T(128)S(1)} %copy-done.3, bf16[256,128,128]{2,1,0:T(8,128)(2,1)} %bitcast.7, bf16[16,512,512]{2,1,0:T(8,128)(2,1)} %get-tuple-element.8.metric_ref), custom_call_target="tpu_custom_call" | custom-call | tf_op jit(solution)/shard_map/apply_metric/pallas_call | solution.py:114
  139.5 102.7 %give_back.1 = f32[32,128,128]{2,1,0:T(8,128)S(1)} custom-call(s32[256]{0:T(256)S(1)} %reshape.54.perm_ref, s32[256]{0:T(256)S(1)} %reshape.55.same_ref, s32[128]{0:T(128)S(1)} %max.12.last_ref, s32[128]{0:T(128)S(1)} %reshape.59.has_ref, bf16[32,8,128,128]{3,2,1,0:T(8,128)(2,1)} %bitcast.6, bf16[32,128,128]{2,1,0:T(8,128)(2,1)S(1)} %copy-done.1), custom_call_target="tpu_custom_call" | custom-call | tf_op jit(solution)/shard_map/give_back/pallas_call | solution.py:468
  242.3 1.3 copy.18
  (16 shorter events, 0.3 us)
Async XLA Ops:
  0.0 119.8 %copy-start.3 = (s32[16]{0:T(128)S(1)}, s32[16]{0:T(128)}, u32[]{:S(2)}) copy-start(s32[16]{0:T(128)} %counts_ref.1) | copy-start | bytes 196
  2.9 9.9 %all-to-all-start = ((s32[8,4,8]{2,1,0:T(4,128)}), s32[8,4,8]{2,1,0:T(4,128)S(1)}, u32[]{:S(2)}, u32[]{:S(2)}) async-start(s32[8,4,8]{2,1,0:T(4,128)} %bitcast), calls=%async_computation | async-start | bytes 32768 | tf_op jit(solution)/shard_map/all_to_all | solution.py:534
  14.4 1.2 copy-start
  15.6 0.7 copy-start.2
  119.8 19.7 %copy-start.1 = (bf16[32,128,128]{2,1,0:T(8,128)(2,1)S(1)}, bf16[32,128,128]{2,1,0:T(8,128)(2,1)}, u32[]{:S(2)}) copy-start(bf16[32,128,128]{2,1,0:T(8,128)(2,1)} %prev_ref.1) | copy-start | bytes 3145732

commit v3 on v2

--- a/solution.py
+++ b/solution.py
@@ -89,23 +89,33 @@
 def apply_kernel(listed, pos_ref, counts_ref, fetched_ref, metric_ref, out_ref, dmat):
     width = fetched_ref.shape[1]
     b = pl.program_id(0)
-    count = counts_ref[b]
-    for i in range(listed):
-        for j in range(listed):
-            live = max(i, j) < count
-            where = pos_ref[b * listed * listed + i * listed + j]
-            tile = fetched_ref[where]
-            dmat[i * width : (i + 1) * width, j * width : (j + 1) * width] = jnp.where(
-                live, tile, jnp.zeros_like(tile)
-            )
-    parts = jnp.dot(metric_ref[...], dmat[...], preferred_element_type=jnp.float32)
-    for i in range(listed):
-        for j in range(listed):
-            live = max(i, j) < count
-            where = pos_ref[b * listed * listed + i * listed + j]
-            part = parts[i * width : (i + 1) * width, j * width : (j + 1) * width]
-            part = part.astype(jnp.bfloat16)
-            out_ref[where] = jnp.where(live, part, jnp.zeros_like(part))
+    count = jnp.clip(counts_ref[b], 0, listed)
+
+    def at(i, j):
+        return pos_ref[b * listed * listed + i * listed + j]
+
+    def live(size):
+        for i in range(size):
+            for j in range(size):
+                dmat[i * width : (i + 1) * width, j * width : (j + 1) * width] = fetched_ref[at(i, j)]
+        span = size * width
+        for i in range(size):
+            parts = jnp.dot(
+                metric_ref[i * width : (i + 1) * width, :span], dmat[:span, :span], preferred_element_type=jnp.float32
+            ).astype(jnp.bfloat16)
+            for j in range(size):
+                out_ref[at(i, j)] = parts[:, j * width : (j + 1) * width]
+
+    def branch(size):
+        if size:
+            live(size)
+        for i in range(listed):
+            for j in range(listed):
+                if max(i, j) >= size:
+                    out_ref[at(i, j)] = jnp.zeros((width, width), jnp.bfloat16)
+
+    for size in range(listed + 1):
+        pl.when(count == size)(functools.partial(branch, size))
 
 
 def apply_metric(pos, counts, fetched, metric):
@@ -186,16 +196,49 @@
     pl.semaphore_wait(barrier, plane - 1 + jnp.where(z > 0, 1, 0) + jnp.where(z < line - 1, 1, 0))
 
 
+def slot_tables(asked_ref, tables_ref, line, capacity):
+    entries = tables_ref.shape[2]
+    row = lax.broadcasted_iota(jnp.int32, (entries, entries), 0)
+    column = lax.broadcasted_iota(jnp.int32, (entries, entries), 1)
+
+    def ones(mask):
+        return jnp.where(mask, 1.0, 0.0)
+
+    for source in range(line):
+
+        def spread(e, carry):
+            down, across = carry
+            slot = asked_ref[e // capacity, 0, source * capacity + e % capacity]
+            return jnp.where(row == e, slot, down), jnp.where(column == e, slot, across)
+
+        zero = jnp.zeros((entries, entries), jnp.int32)
+        mine, other = lax.fori_loop(0, entries, spread, (zero, zero))
+        twin = (other == mine) & (column < row)
+        place = jnp.sum(ones((other < mine) | twin), axis=1, keepdims=True)
+        shared = jnp.max(ones(twin), axis=1, keepdims=True)
+        at = place == column.astype(jnp.float32)
+        tables_ref[source, 0:1, :] = jnp.sum(jnp.where(at, row.astype(jnp.float32), 0.0), axis=0, keepdims=True).astype(jnp.int32)
+        tables_ref[source, 1:2, :] = jnp.sum(jnp.where(at, shared, 0.0), axis=0, keepdims=True).astype(jnp.int32)
+        upto = jnp.sum(ones(mine <= column), axis=0, keepdims=True)
+        tables_ref[source, 2:3, :] = jnp.maximum(upto - 1.0, 0.0).astype(jnp.int32)
+        tables_ref[source, 3:4, :] = jnp.max(ones(mine == column), axis=0, keepdims=True).astype(jnp.int32)
+        tables_ref[source, 4:8, :] = jnp.zeros((4, entries), jnp.int32)
+
+
 def fetch_kernel(
-    plane, line, asked_ref, scales_ref, dens_ref, colloc_ref, coords_ref, weights_ref, fetched_ref, metric_ref,
-    *scratch
+    plane, line, wanted_ref, scales_ref, dens_ref, colloc_hbm, coords_ref, weights_ref, fetched_ref, metric_hbm,
+    tables_ref, *scratch
 ):
-    pools, (stage, hop_send, hop_recv, local_sem, send_sem, recv_sem) = scratch[:line], scratch[line:]
+    pools, rest = scratch[:line], scratch[line:]
+    stage, colloc_ref, metric_ref, asked_vmem, asked_ref = rest[:5]
+    in_sem, out_sem, smem_sem, ask_send, ask_recv, hop_send, hop_recv, local_sem, send_sem, recv_sem = rest[5:]
     capacity = fetched_ref.shape[1]
     stored = dens_ref.shape[0]
     batches = colloc_ref.shape[0]
     me = lax.axis_index("grid")
     z, q = me // plane, lax.rem(me, plane)
+    load = pltpu.make_async_copy(colloc_hbm, colloc_ref, in_sem)
+    load.start()
 
     def scale(t, carry):
         pools[0][t] = (dens_ref[t].astype(jnp.float32) * scales_ref[t]).astype(jnp.bfloat16)
@@ -246,13 +289,13 @@
     def serve(slot):
         if slot:
             hop(slot - 1, True).wait_recv()
-        hops(slot, lambda copy: copy.start())
+            hops(slot, lambda copy: copy.start())
         source = lax.rem(z - slot + line, line)
 
         def fill(k):
-            base = (lax.rem(q + k, plane) * line + source) * capacity
+            to = lax.rem(q + k, plane)
             for r in range(capacity):
-                stage[slot, k, r] = pools[slot][asked_ref[base + r]]
+                stage[slot, k, r] = pools[slot][asked_ref[to, 0, source * capacity + r]]
 
         def one(k, carry):
             fill(k)
@@ -270,14 +313,44 @@
 
         lax.fori_loop(first, last, one, 0)
 
+    def ask(k):
+        return pltpu.make_async_remote_copy(
+            src_ref=wanted_ref.at[lax.rem(q + k, plane)],
+            dst_ref=asked_vmem.at[q],
+            send_sem=ask_send.at[k],
+            recv_sem=ask_recv.at[k],
+            device_id=mate(z, lax.rem(q + k, plane), plane),
+            device_id_type=pl.DeviceIdType.MESH,
+        )
+
+    def store_metrics(d):
+        rows = pl.ds(batches * (d - 1) // (line - 1), batches * d // (line - 1) - batches * (d - 1) // (line - 1))
+        return pltpu.make_async_copy(metric_ref.at[rows], metric_hbm.at[rows], out_sem.at[d])
+
+    for k in range(1, plane):
+        ask(k).start()
+    own = pltpu.make_async_copy(wanted_ref.at[q], asked_vmem.at[q], ask_send.at[0])
+    own.start()
+    hops(0, lambda copy: copy.start())
+    own.wait()
+    for k in range(1, plane):
+        ask(k).wait()
+    scalars = pltpu.make_async_copy(asked_vmem, asked_ref, smem_sem)
+    scalars.start()
+    scalars.wait()
     serve(0)
+    slot_tables(asked_ref, tables_ref, line, capacity)
+    load.wait()
     for d in range(1, line):
         metrics(batches * (d - 1) // (line - 1), batches * d // (line - 1))
+        store_metrics(d).start()
         if 2 * d == line:
             serve(d)
         else:
             pl.when(z >= d)(functools.partial(serve, d))
             pl.when(z + d < line)(functools.partial(serve, line - d))
+    for d in range(1, line):
+        store_metrics(d).wait()
     for slot in range(line):
         hops(slot, lambda copy: copy.wait_send())
         to_self(slot).wait()
@@ -289,21 +362,32 @@
         lax.fori_loop(1, plane, finish, 0)
 
 
-def fetch(asked, scales, dens, collocation, coords, weights, plane, line, capacity):
+def fetch(wanted, scales, dens, collocation, coords, weights, plane, line, capacity):
     stored, width, _ = dens.shape
     per_dev, points, funcs = collocation.shape
     vmem, smem = pl.BlockSpec(memory_space=pltpu.VMEM), pl.BlockSpec(memory_space=pltpu.SMEM)
+    hbm = pl.BlockSpec(memory_space=pl.ANY)
     return pl.pallas_call(
         functools.partial(fetch_kernel, plane, line),
         out_shape=(
             jax.ShapeDtypeStruct((line * plane, capacity, width, width), jnp.bfloat16),
             jax.ShapeDtypeStruct((per_dev, funcs, funcs), jnp.bfloat16),
-        ),
-        in_specs=[smem, smem, vmem, vmem, vmem, vmem],
-        out_specs=(pl.BlockSpec(memory_space=pl.ANY), vmem),
+            jax.ShapeDtypeStruct((line, 8, plane * capacity), jnp.int32),
+        ),
+        in_specs=[vmem, smem, vmem, hbm, vmem, vmem],
+        out_specs=(hbm, hbm, vmem),
         scratch_shapes=[pltpu.VMEM((stored, width, width), jnp.bfloat16)] * line
         + [
             pltpu.VMEM((line, plane, capacity, width, width), jnp.bfloat16),
+            pltpu.VMEM((per_dev, points, funcs), jnp.bfloat16),
+            pltpu.VMEM((per_dev, funcs, funcs), jnp.bfloat16),
+            pltpu.VMEM(wanted.shape, jnp.int32),
+            pltpu.SMEM(wanted.shape, jnp.int32),
+            pltpu.SemaphoreType.DMA,
+            pltpu.SemaphoreType.DMA((line,)),
+            pltpu.SemaphoreType.DMA,
+            pltpu.SemaphoreType.DMA((plane,)),
+            pltpu.SemaphoreType.DMA((plane,)),
             pltpu.SemaphoreType.DMA((line + 1,)),
             pltpu.SemaphoreType.DMA((line,)),
             pltpu.SemaphoreType.DMA((line,)),
@@ -314,11 +398,11 @@
             collective_id=0, has_side_effects=True, vmem_limit_bytes=VMEM_BYTES
         ),
         name="fetch",
-    )(asked, scales, dens, collocation, coords, weights[:, None, :])
+    )(wanted, scales, dens, collocation, coords, weights[:, None, :])
 
 
 def return_kernel(
-    plane, line, perm_ref, same_ref, last_ref, has_ref, outgoing_ref, prev_ref, out_ref, *scratch
+    plane, line, tables_ref, outgoing_ref, prev_ref, out_ref, *scratch
 ):
     received, rest = scratch[:line], scratch[line:]
     running, part, inbox, hop_send, hop_recv, local_sem, send_sem, recv_sem = rest
@@ -389,8 +473,8 @@
         row = lax.rem(z + order[p], line)
 
         def one(k, total):
-            tile = received[p][perm_ref[row * entries + k]].astype(jnp.float32)
-            total = jnp.where(same_ref[row * entries + k] != 0, total, 0.0) + tile
+            tile = received[p][tables_ref[row, 0, k]].astype(jnp.float32)
+            total = jnp.where(tables_ref[row, 1, k] != 0, total, 0.0) + tile
             running[k] = total
             return total
 
@@ -398,7 +482,7 @@
 
     def slot_sum(p, t):
         row = lax.rem(z + order[p], line)
-        return jnp.where(has_ref[row * stored + t] != 0, running[last_ref[row * stored + t]], 0.0)
+        return jnp.where(tables_ref[row, 3, t] != 0, running[tables_ref[row, 2, t]], 0.0)
 
     def each(body):
         def one(t, carry):
@@ -468,7 +552,7 @@
     return pl.pallas_call(
         functools.partial(return_kernel, plane, line),
         out_shape=jax.ShapeDtypeStruct((stored, width, width), jnp.float32),
-        in_specs=[smem, smem, smem, smem, pl.BlockSpec(memory_space=pl.ANY), vmem],
+        in_specs=[smem, pl.BlockSpec(memory_space=pl.ANY), vmem],
         out_specs=vmem,
         scratch_shapes=[pltpu.VMEM((plane * capacity, width, width), jnp.bfloat16)] * line
         + [
@@ -485,26 +569,7 @@
             collective_id=1, has_side_effects=True, vmem_limit_bytes=VMEM_BYTES
         ),
         name="give_back",
-    )(*tables, outgoing, prev)
-
-
-def slot_tables(asked, stored):
-    entries = asked.shape[1]
-    index = jnp.arange(entries, dtype=jnp.int32)
-    earlier = (asked[:, None, :] < asked[:, :, None]) | (
-        (asked[:, None, :] == asked[:, :, None]) & (index[None, None, :] < index[None, :, None])
-    )
-    place = jnp.sum(earlier.astype(jnp.int32), axis=2)
-    at = place[:, None, :] == index[None, :, None]
-    perm = jnp.sum(jnp.where(at, index[None, None, :], 0), axis=2)
-    shared = jnp.any(
-        (asked[:, None, :] == asked[:, :, None]) & (index[None, None, :] < index[None, :, None]), axis=2
-    )
-    same = jnp.sum((at & shared[:, None, :]).astype(jnp.int32), axis=2)
-    slot = jnp.arange(stored, dtype=jnp.int32)[None, :, None]
-    last = jnp.maximum(jnp.sum((asked[:, None, :] <= slot).astype(jnp.int32), axis=2) - 1, 0)
-    has = jnp.any(asked[:, None, :] == slot, axis=2).astype(jnp.int32)
-    return tuple(table.reshape(-1) for table in (perm, same, last, has))
+    )(tables, outgoing, prev)
 
 
 def shards(collocation, coords, weights, owners, slots, counts, dens_tiles, dens_scales, fock_prev):
@@ -528,15 +593,11 @@
     ).astype(jnp.int32)
     plane = 8
     line = npeer // plane
-    if line == 4:
-        wanted = requests.reshape(line, plane, capacity).transpose(1, 0, 2)
-        groups = [[z * plane + k for k in range(plane)] for z in range(line)]
-        asked = lax.all_to_all(
-            wanted, "grid", split_axis=0, concat_axis=0, tiled=True, axis_index_groups=groups
-        )
-        tables = slot_tables(asked.transpose(1, 0, 2).reshape(line, plane * capacity), dens_tiles.shape[0])
-        fetched, metric = fetch(
-            asked.reshape(-1), dens_scales, dens_tiles, collocation, coords, weights, plane, line, capacity
+    if line == 4 and plane * capacity >= dens_tiles.shape[0]:
+        wanted = requests.reshape(line, plane, capacity).transpose(1, 0, 2).reshape(plane, 1, line * capacity)
+        wanted = jnp.pad(wanted, ((0, 0), (0, 7), (0, 128 - line * capacity)))
+        fetched, metric, tables = fetch(
+            wanted, dens_scales, dens_tiles, collocation, coords, weights, plane, line, capacity
         )
         outgoing = apply_metric(pos, counts, fetched.reshape(entries, width, width), metric)
         return give_back(tables, outgoing.reshape(npeer, capacity, width, width), fock_prev, plane, line)

time: 245 us -> 233 us (0.951)
  starting transfers between devices: 5.17 us -> 0 us
  waiting for transfers between devices: 2.98 us -> 0 us
    all_to_all x1 -> x0, starting transfers between devices: 5.17 us -> none  [shards(): lax.all_to_all(wanted, 'grid', split_axis=0, concat_axis=0, tiled=True, a...]
    pallas_call x1, Pallas kernels: 103 us -> 106 us  [give_back(): pl.pallas_call(functools.partial(return_kernel, plane, line), out_shape=j...]
    all_to_all x1 -> x0, waiting for transfers between devices: 2.98 us -> none  [shards(): lax.all_to_all(wanted, 'grid', split_axis=0, concat_axis=0, tiled=True, a...]
    pallas_call x1, Pallas kernels: 104 us -> 101 us  [fetch(): pl.pallas_call(functools.partial(fetch_kernel, plane, line), out_shape=(j...]
  transfers between devices with their start and end apart: 1 -> 0, of which waited for: 1 -> 0; matrix products, arithmetic and copies ran while one was open for 1% -> 0% of each run, Pallas kernels for 0% -> 0%
where the time goes in v3:
time: 233 us
  Pallas kernels  226 us (97%)
  local copies, waits for them, and re-layouts  6.79 us (3%)
    pallas_call x1, Pallas kernels, give_back(): pl.pallas_call(functools.partial(return_kernel, plane, line), out_shape=j...  106 us
    pallas_call x1, Pallas kernels, fetch(): pl.pallas_call(functools.partial(fetch_kernel, plane, line), out_shape=(j...  101 us
    pallas_call x1, Pallas kernels, apply_metric(): pl.pallas_call(functools.partial(apply_kernel, funcs // width), out_shape...  18.8 us

profile of v3, /device:TPU:0, one launch (start us, length us, event | category | flops | bytes accessed | tf_op | source)
XLA Modules:
  0.0 233.4 jit_solution(12837501609912793878)
XLA Ops:
  0.0 0.0 copy-start.3
  0.0 0.8 eq.28
  0.8 0.8 broadcast_in_dim.29
  1.6 0.3 fusion
  1.9 0.3 convolution_convert_fusion
  2.2 0.1 reshape.18
  2.2 0.1 copy.10
  2.3 0.1 reshape.19
  2.4 0.8 broadcast_in_dim.32.weights_ref
  3.2 1.0 copy.11.coords_ref
  4.2 0.0 copy-start
  4.2 1.2 copy-done
  5.4 0.0 copy-start.2
  5.4 0.7 copy-done.2
  6.1 100.8 %fetch.1 = (bf16[32,8,128,128]{3,2,1,0:T(8,128)(2,1)}, bf16[16,512,512]{2,1,0:T(8,128)(2,1)}, s32[4,8,64]{2,1,0:T(8,128)S(1)}) custom-call(s32[8,8,128]{2,1,0:T(8,128)S(1)} %pad.4.wanted_ref, f32[32]{0:T(128)S(1)} %copy-done.2, bf16[32,128,128]{2,1,0:T(8,128)(2,1)S(1)} %copy-done, bf16[16,512,512]{2,1,0:T(8,128)(2,1)} %colloc_hbm.1, ...), custom_call_target="tpu_custom_call" | custom-call | tf_op jit(solution)/shard_map/fetch/pallas_call | solution.py:370
  106.9 0.0 copy-done.3
  106.9 0.0 copy-start.1
  106.9 18.8 %apply_metric.1 = bf16[256,128,128]{2,1,0:T(8,128)(2,1)} custom-call(s32[256]{0:T(256)S(1)} %multiply_add_fusion.pos_ref, s32[16]{0:T(128)S(1)} %copy-done.3, bf16[256,128,128]{2,1,0:T(8,128)(2,1)} %bitcast.6, bf16[16,512,512]{2,1,0:T(8,128)(2,1)} %get-tuple-element.10.metric_ref), custom_call_target="tpu_custom_call" | custom-call | tf_op jit(solution)/shard_map/apply_metric/pallas_call | solution.py:124
  125.7 0.0 copy-done.1
  125.7 106.3 %give_back.1 = f32[32,128,128]{2,1,0:T(8,128)S(1)} custom-call(s32[4,8,64]{2,1,0:T(8,128)S(1)} %get-tuple-element.8.tables_ref, bf16[32,8,128,128]{3,2,1,0:T(8,128)(2,1)} %bitcast.5, bf16[32,128,128]{2,1,0:T(8,128)(2,1)S(1)} %copy-done.1), custom_call_target="tpu_custom_call" | custom-call | tf_op jit(solution)/shard_map/give_back/pallas_call | solution.py:552
  232.0 1.3 copy.13
  (4 shorter events, 0.0 us)
Async XLA Ops:
  0.0 106.9 %copy-start.3 = (s32[16]{0:T(128)S(1)}, s32[16]{0:T(128)}, u32[]{:S(2)}) copy-start(s32[16]{0:T(128)} %counts_ref.1) | copy-start | bytes 196
  4.2 1.2 copy-start
  5.4 0.7 copy-start.2
  106.9 18.8 %copy-start.1 = (bf16[32,128,128]{2,1,0:T(8,128)(2,1)S(1)}, bf16[32,128,128]{2,1,0:T(8,128)(2,1)}, u32[]{:S(2)}) copy-start(bf16[32,128,128]{2,1,0:T(8,128)(2,1)} %prev_ref.1) | copy-start | bytes 3145732

commit v4 on v3

--- a/solution.py
+++ b/solution.py
@@ -8,7 +8,7 @@
 from jax.sharding import PartitionSpec as P
 
 SOFTEN = 0.5
-VMEM_BYTES = 48 * 2**20
+VMEM_BYTES = 56 * 2**20
 
 
 def metric_kernel(colloc_ref, coords_ref, weights_ref, metric_ref):
@@ -226,13 +226,14 @@
 
 
 def fetch_kernel(
-    plane, line, wanted_ref, scales_ref, dens_ref, colloc_hbm, coords_ref, weights_ref, fetched_ref, metric_hbm,
-    tables_ref, *scratch
+    plane, line, wanted_ref, scales_ref, pos_ref, inverse_ref, counts_ref, dens_ref, colloc_hbm, coords_ref,
+    weights_ref, outgoing_ref, tables_ref, *scratch
 ):
     pools, rest = scratch[:line], scratch[line:]
-    stage, colloc_ref, metric_ref, asked_vmem, asked_ref = rest[:5]
-    in_sem, out_sem, smem_sem, ask_send, ask_recv, hop_send, hop_recv, local_sem, send_sem, recv_sem = rest[5:]
-    capacity = fetched_ref.shape[1]
+    stage, fetched_ref, parts_ref, dmat_ref, colloc_ref, metric_ref, asked_vmem, asked_ref = rest[:8]
+    in_sem, out_sem, smem_sem, ask_send, ask_recv, hop_send, hop_recv, local_sem, send_sem, recv_sem = rest[8:]
+    capacity, width = stage.shape[2:4]
+    listed = colloc_ref.shape[2] // width
     stored = dens_ref.shape[0]
     batches = colloc_ref.shape[0]
     me = lax.axis_index("grid")
@@ -275,7 +276,7 @@
         owner = lax.rem(z - slot + line, line) * plane + q
         return pltpu.make_async_remote_copy(
             src_ref=stage.at[slot, k],
-            dst_ref=fetched_ref.at[owner],
+            dst_ref=fetched_ref.at[pl.ds(owner * capacity, capacity)],
             send_sem=send_sem.at[slot, k],
             recv_sem=recv_sem.at[slot, k],
             device_id=mate(z, lax.rem(q + k, plane), plane),
@@ -284,7 +285,9 @@
 
     def to_self(slot):
         owner = lax.rem(z - slot + line, line) * plane + q
-        return pltpu.make_async_copy(stage.at[slot, 0], fetched_ref.at[owner], local_sem.at[slot])
+        return pltpu.make_async_copy(
+            stage.at[slot, 0], fetched_ref.at[pl.ds(owner * capacity, capacity)], local_sem.at[slot]
+        )
 
     def serve(slot):
         if slot:
@@ -308,7 +311,7 @@
 
     def metrics(first, last):
         def one(b, carry):
-            metric_kernel(colloc_ref.at[b], coords_ref.at[b], weights_ref.at[b], metric_ref.at[b])
+            metric_kernel(colloc_ref.at[b], coords_ref.at[b], weights_ref.at[pl.ds(b, 1)], metric_ref.at[b])
             return carry
 
         lax.fori_loop(first, last, one, 0)
@@ -322,10 +325,6 @@
             device_id=mate(z, lax.rem(q + k, plane), plane),
             device_id_type=pl.DeviceIdType.MESH,
         )
-
-    def store_metrics(d):
-        rows = pl.ds(batches * (d - 1) // (line - 1), batches * d // (line - 1) - batches * (d - 1) // (line - 1))
-        return pltpu.make_async_copy(metric_ref.at[rows], metric_hbm.at[rows], out_sem.at[d])
 
     for k in range(1, plane):
         ask(k).start()
@@ -343,14 +342,11 @@
     load.wait()
     for d in range(1, line):
         metrics(batches * (d - 1) // (line - 1), batches * d // (line - 1))
-        store_metrics(d).start()
         if 2 * d == line:
             serve(d)
         else:
             pl.when(z >= d)(functools.partial(serve, d))
             pl.when(z + d < line)(functools.partial(serve, line - d))
-    for d in range(1, line):
-        store_metrics(d).wait()
     for slot in range(line):
         hops(slot, lambda copy: copy.wait_send())
         to_self(slot).wait()
@@ -361,8 +357,48 @@
 
         lax.fori_loop(1, plane, finish, 0)
 
-
-def fetch(wanted, scales, dens, collocation, coords, weights, plane, line, capacity):
+    def product(b, buffer):
+        count = counts_ref[b]
+        for i in range(listed):
+            for j in range(listed):
+                tile = fetched_ref[pos_ref[(b * listed + i) * listed + j]]
+                dmat_ref[buffer, i * width : (i + 1) * width, j * width : (j + 1) * width] = jnp.where(
+                    max(i, j) < count, tile, jnp.zeros_like(tile)
+                )
+        parts = jnp.dot(metric_ref[b], dmat_ref[buffer], preferred_element_type=jnp.float32)
+        for i in range(listed):
+            for j in range(listed):
+                part = parts[i * width : (i + 1) * width, j * width : (j + 1) * width].astype(jnp.bfloat16)
+                parts_ref[(b * listed + i) * listed + j] = jnp.where(max(i, j) < count, part, jnp.zeros_like(part))
+
+    buffers = dmat_ref.shape[0]
+
+    def products(step, carry):
+        for buffer in range(buffers):
+            product(step * buffers + buffer, buffer)
+        return carry
+
+    lax.fori_loop(0, batches // buffers, products, 0)
+
+    def put_out(source):
+        return pltpu.make_async_copy(
+            stage.at[source], outgoing_ref.at[pl.ds(source * plane, plane)], out_sem.at[source]
+        )
+
+    for source in range(line):
+
+        def arrange(lane, carry):
+            for r in range(capacity):
+                stage[source, lane, r] = parts_ref[inverse_ref[(source * plane + lane) * capacity + r]]
+            return carry
+
+        lax.fori_loop(0, plane, arrange, 0)
+        put_out(source).start()
+    for source in range(line):
+        put_out(source).wait()
+
+
+def fetch(wanted, scales, pos, inverse, counts, dens, collocation, coords, weights, plane, line, capacity):
     stored, width, _ = dens.shape
     per_dev, points, funcs = collocation.shape
     vmem, smem = pl.BlockSpec(memory_space=pltpu.VMEM), pl.BlockSpec(memory_space=pltpu.SMEM)
@@ -371,14 +407,16 @@
         functools.partial(fetch_kernel, plane, line),
         out_shape=(
             jax.ShapeDtypeStruct((line * plane, capacity, width, width), jnp.bfloat16),
-            jax.ShapeDtypeStruct((per_dev, funcs, funcs), jnp.bfloat16),
             jax.ShapeDtypeStruct((line, 8, plane * capacity), jnp.int32),
         ),
-        in_specs=[vmem, smem, vmem, hbm, vmem, vmem],
-        out_specs=(hbm, hbm, vmem),
+        in_specs=[vmem, smem, smem, smem, smem, vmem, hbm, vmem, vmem],
+        out_specs=(hbm, vmem),
         scratch_shapes=[pltpu.VMEM((stored, width, width), jnp.bfloat16)] * line
         + [
             pltpu.VMEM((line, plane, capacity, width, width), jnp.bfloat16),
+            pltpu.VMEM((line * plane * capacity, width, width), jnp.bfloat16),
+            pltpu.VMEM((line * plane * capacity, width, width), jnp.bfloat16),
+            pltpu.VMEM((2 - per_dev % 2, funcs, funcs), jnp.bfloat16),
             pltpu.VMEM((per_dev, points, funcs), jnp.bfloat16),
             pltpu.VMEM((per_dev, funcs, funcs), jnp.bfloat16),
             pltpu.VMEM(wanted.shape, jnp.int32),
@@ -398,7 +436,7 @@
             collective_id=0, has_side_effects=True, vmem_limit_bytes=VMEM_BYTES
         ),
         name="fetch",
-    )(wanted, scales, dens, collocation, coords, weights[:, None, :])
+    )(wanted, scales, pos, inverse, counts, dens, collocation, coords, weights)
 
 
 def return_kernel(
@@ -478,7 +516,7 @@
             running[k] = total
             return total
 
-        lax.fori_loop(0, entries, one, jnp.zeros((width, width), jnp.float32))
+        lax.fori_loop(0, entries, one, jnp.zeros((width, width), jnp.float32), unroll=4)
 
     def slot_sum(p, t):
         row = lax.rem(z + order[p], line)
@@ -489,7 +527,7 @@
             body(t)
             return carry
 
-        lax.fori_loop(0, stored, one, 0)
+        lax.fori_loop(0, stored, one, 0, unroll=4)
 
     exchange(0)
     exchange(1)
@@ -596,11 +634,16 @@
     if line == 4 and plane * capacity >= dens_tiles.shape[0]:
         wanted = requests.reshape(line, plane, capacity).transpose(1, 0, 2).reshape(plane, 1, line * capacity)
         wanted = jnp.pad(wanted, ((0, 0), (0, 7), (0, 128 - line * capacity)))
-        fetched, metric, tables = fetch(
-            wanted, dens_scales, dens_tiles, collocation, coords, weights, plane, line, capacity
-        )
-        outgoing = apply_metric(pos, counts, fetched.reshape(entries, width, width), metric)
-        return give_back(tables, outgoing.reshape(npeer, capacity, width, width), fock_prev, plane, line)
+        index = jnp.arange(entries, dtype=jnp.int32)[:, None]
+        numbered = jnp.where(rank[:, None] == jnp.arange(capacity, dtype=jnp.int32)[None, :], index, 0)
+        inverse = jnp.dot(
+            onehot.T.astype(jnp.float32), numbered.astype(jnp.float32), precision=lax.Precision.HIGHEST
+        ).astype(jnp.int32)
+        outgoing, tables = fetch(
+            wanted, dens_scales, pos, inverse.reshape(-1), counts, dens_tiles, collocation, coords, weights,
+            plane, line, capacity,
+        )
+        return give_back(tables, outgoing, fock_prev, plane, line)
     asked = lax.all_to_all(requests, "grid", split_axis=0, concat_axis=0, tiled=True).reshape(-1)
     chunk = 16
     tiles = pick(asked, dens_scales, dens_tiles, chunk)

time: 233 us -> 227 us (0.974)
  Pallas kernels: 226 us -> 218 us
    pallas_call x1 -> x0, Pallas kernels: 18.8 us -> none  [apply_metric(): pl.pallas_call(functools.partial(apply_kernel, funcs // width), out_shape...]
    pallas_call x1, Pallas kernels: 101 us -> 112 us  [fetch(): pl.pallas_call(functools.partial(fetch_kernel, plane, line), out_shape=(j...]
    unnamed x10 -> x2, local copies, waits for them, and re-layouts: 4.17 us -> 4.75 us
where the time goes in v4:
time: 227 us
  Pallas kernels  218 us (96%)
  local copies, waits for them, and re-layouts  7.88 us (3%)
    pallas_call x1, Pallas kernels, fetch(): pl.pallas_call(functools.partial(fetch_kernel, plane, line), out_shape=(j...  112 us
    pallas_call x1, Pallas kernels, give_back(): pl.pallas_call(functools.partial(return_kernel, plane, line), out_shape=j...  106 us
    unnamed x2, local copies, waits for them, and re-layouts  4.75 us

profile of v4, /device:TPU:0, one launch (start us, length us, event | category | flops | bytes accessed | tf_op | source)
XLA Modules:
  0.0 227.1 jit_solution(18271300343556132255)
XLA Ops:
  0.0 0.8 eq.14
  0.8 0.8 broadcast_in_dim.35
  1.6 0.3 fusion
  1.8 0.5 multiply_add_fusion.pos_ref
  2.4 0.3 convolution_convert_fusion.1
  2.7 0.3 convolution_convert_fusion
  3.0 0.1 copy.13
  3.1 0.6 reshape.17.inverse_ref
  3.7 0.1 reshape.15
  3.8 0.1 copy.12
  3.9 0.1 reshape.16
  3.9 0.6 pad.4.wanted_ref
  4.6 1.6 copy.14.coords_ref
  6.2 112.0 %fetch.1 = (bf16[32,8,128,128]{3,2,1,0:T(8,128)(2,1)}, s32[4,8,64]{2,1,0:T(8,128)}) custom-call(s32[8,8,128]{2,1,0:T(8,128)} %pad.4.wanted_ref, f32[32]{0:T(128)} %scales_ref.1, s32[256]{0:T(256)} %multiply_add_fusion.pos_ref, s32[256]{0:T(256)} %reshape.17.inverse_ref, s32[16]{0:T(128)} %counts_ref.1, bf16[32,128,128]{2,1,0:T(8,128)(2,1)} %dens_ref.1, ...), custom_call_target="tpu_custom_call" | custom-call | tf_op jit(solution)/shard_map/fetch/pallas_call | solution.py:406
  118.2 105.7 %give_back.1 = f32[32,128,128]{2,1,0:T(8,128)} custom-call(s32[4,8,64]{2,1,0:T(8,128)} %get-tuple-element.7.tables_ref, bf16[32,8,128,128]{3,2,1,0:T(8,128)(2,1)} %get-tuple-element.8.outgoing_ref, bf16[32,128,128]{2,1,0:T(8,128)(2,1)} %prev_ref.1), custom_call_target="tpu_custom_call" | custom-call | tf_op jit(solution)/shard_map/give_back/pallas_call | solution.py:590
  224.0 3.1 %copy.16 = f32[32,128,128]{2,1,0:T(8,128)} copy(f32[32,128,128]{2,1,0:T(8,128)} %give_back.1) | data formatting | bytes 4194304
  (2 shorter events, 0.0 us)

commit v5 on v4

--- a/solution.py
+++ b/solution.py
@@ -8,7 +8,7 @@
 from jax.sharding import PartitionSpec as P
 
 SOFTEN = 0.5
-VMEM_BYTES = 56 * 2**20
+VMEM_BYTES = 62 * 2**20
 
 
 def metric_kernel(colloc_ref, coords_ref, weights_ref, metric_ref):
@@ -225,21 +225,168 @@
         tables_ref[source, 4:8, :] = jnp.zeros((4, entries), jnp.int32)
 
 
-def fetch_kernel(
+def give_back(
+    z, q, plane, line, arrange, tables_ref, stage, prev_ref, out_ref, received, part, running, inbox,
+    hop_send, hop_recv, local_sem, send_sem, recv_sem
+):
+    capacity, width = stage.shape[2:4]
+    stored = prev_ref.shape[0]
+    entries = plane * capacity
+    order = [jnp.where(z == 0, line - 1 - p, jnp.where(z == line - 1, (p + 1) % line, (2, 1, 3, 0)[p])) for p in range(line)]
+
+    def to_mate(p, k):
+        to = lax.rem(q + k, plane)
+        return pltpu.make_async_remote_copy(
+            src_ref=stage.at[lax.rem(z + order[p], line), to],
+            dst_ref=received[p].at[pl.ds(q * capacity, capacity)],
+            send_sem=send_sem.at[p, k],
+            recv_sem=recv_sem.at[p, k],
+            device_id=mate(z, to, plane),
+            device_id_type=pl.DeviceIdType.MESH,
+        )
+
+    def to_self(p):
+        return pltpu.make_async_copy(
+            stage.at[lax.rem(z + order[p], line), q],
+            received[p].at[pl.ds(q * capacity, capacity)],
+            local_sem.at[p],
+        )
+
+    def exchange(p):
+        arrange(lax.rem(z + order[p], line))
+
+        def one(k, carry):
+            to_mate(p, k).start()
+            return carry
+
+        lax.fori_loop(1, plane, one, 0)
+        to_self(p).start()
+
+    def hop(p, up):
+        to = order[p] - 1 if up else order[p] + 1
+        return pltpu.make_async_remote_copy(
+            src_ref=part[p],
+            dst_ref=inbox.at[to],
+            send_sem=hop_send.at[p],
+            recv_sem=hop_recv.at[to],
+            device_id=mate(z + 1 if up else z - 1, q, plane),
+            device_id_type=pl.DeviceIdType.MESH,
+        )
+
+    def arrival(slot):
+        return pltpu.make_async_remote_copy(
+            src_ref=part[0],
+            dst_ref=inbox.at[slot],
+            send_sem=hop_send.at[0],
+            recv_sem=hop_recv.at[slot],
+            device_id=mate(z, lax.rem(q + 1, plane), plane),
+            device_id_type=pl.DeviceIdType.MESH,
+        )
+
+    def gather(p):
+        def finish(k, carry):
+            to_mate(p, k).wait()
+            return carry
+
+        lax.fori_loop(1, plane, finish, 0)
+        to_self(p).wait()
+        if p + 2 < line:
+            exchange(p + 2)
+        row = lax.rem(z + order[p], line)
+
+        def one(k, total):
+            tile = received[p][jnp.clip(tables_ref[row, 0, k], 0, entries - 1)].astype(jnp.float32)
+            total = jnp.where(tables_ref[row, 1, k] != 0, total, 0.0) + tile
+            running[k] = total
+            return total
+
+        lax.fori_loop(0, entries, one, jnp.zeros((width, width), jnp.float32), unroll=4)
+
+    def slot_sum(p, t):
+        row = lax.rem(z + order[p], line)
+        return jnp.where(tables_ref[row, 3, t] != 0, running[jnp.clip(tables_ref[row, 2, t], 0, entries - 1)], 0.0)
+
+    def each(body):
+        def one(t, carry):
+            body(t)
+            return carry
+
+        lax.fori_loop(0, stored, one, 0, unroll=4)
+
+    exchange(0)
+    exchange(1)
+    for p in range(line - 1):
+        gather(p)
+        up = z + order[p] < line
+        feeds = jnp.where(up, z > 0, z < line - 1)
+
+        @pl.when(feeds)
+        def _():
+            arrival(order[p]).wait_recv()
+
+            def body(t):
+                part[p][t] = (slot_sum(p, t) + inbox[order[p], t].astype(jnp.float32)).astype(jnp.bfloat16)
+
+            each(body)
+
+        @pl.when(jnp.logical_not(feeds))
+        def _():
+            def body(t):
+                part[p][t] = slot_sum(p, t).astype(jnp.bfloat16)
+
+            each(body)
+
+        pl.when(up)(lambda: hop(p, True).start())
+        pl.when(jnp.logical_not(up))(lambda: hop(p, False).start())
+    gather(line - 1)
+
+    for slot, there in ((0, z > 0), (line, z < line - 1)):
+
+        @pl.when(there)
+        def _():
+            arrival(slot).wait_recv()
+
+        @pl.when(jnp.logical_not(there))
+        def _():
+            inbox[slot] = jnp.zeros(inbox.shape[1:], inbox.dtype)
+
+    def last(t):
+        total = slot_sum(line - 1, t) + inbox[0, t].astype(jnp.float32) + inbox[line, t].astype(jnp.float32)
+        out_ref[t] = prev_ref[t].astype(jnp.float32) - 0.5 * total
+
+    each(last)
+    for p in range(line - 1):
+        arrival_of = pltpu.make_async_remote_copy(
+            src_ref=part[p],
+            dst_ref=inbox.at[0],
+            send_sem=hop_send.at[p],
+            recv_sem=hop_recv.at[0],
+            device_id=mate(z, lax.rem(q + 1, plane), plane),
+            device_id_type=pl.DeviceIdType.MESH,
+        )
+        arrival_of.wait_send()
+
+
+def exchange_kernel(
     plane, line, wanted_ref, scales_ref, pos_ref, inverse_ref, counts_ref, dens_ref, colloc_hbm, coords_ref,
-    weights_ref, outgoing_ref, tables_ref, *scratch
+    weights_ref, prev_ref, out_ref, *scratch
 ):
-    pools, rest = scratch[:line], scratch[line:]
-    stage, fetched_ref, parts_ref, dmat_ref, colloc_ref, metric_ref, asked_vmem, asked_ref = rest[:8]
-    in_sem, out_sem, smem_sem, ask_send, ask_recv, hop_send, hop_recv, local_sem, send_sem, recv_sem = rest[8:]
+    pools, received, rest = scratch[:line], scratch[line : 2 * line], scratch[2 * line :]
+    stage, fetched_ref, dmat_ref, colloc_ref, metric_ref, asked_vmem, asked_ref, tables_vmem, tables_ref = rest[:9]
+    running, inbox, parts_ref = rest[9:12]
+    in_sem, smem_sem, ask_send, ask_recv, hop_send, hop_recv, local_sem, send_sem, recv_sem = rest[12:21]
+    return_sems = rest[21:]
     capacity, width = stage.shape[2:4]
-    listed = colloc_ref.shape[2] // width
+    listed = colloc_hbm.shape[2] // width
     stored = dens_ref.shape[0]
-    batches = colloc_ref.shape[0]
+    batches = colloc_hbm.shape[0]
     me = lax.axis_index("grid")
     z, q = me // plane, lax.rem(me, plane)
-    load = pltpu.make_async_copy(colloc_hbm, colloc_ref, in_sem)
-    load.start()
+
+    def load(b):
+        return pltpu.make_async_copy(colloc_hbm.at[b], colloc_ref.at[lax.rem(b, 2)], in_sem.at[lax.rem(b, 2)])
+
+    load(0).start()
 
     def scale(t, carry):
         pools[0][t] = (dens_ref[t].astype(jnp.float32) * scales_ref[t]).astype(jnp.bfloat16)
@@ -311,7 +458,13 @@
 
     def metrics(first, last):
         def one(b, carry):
-            metric_kernel(colloc_ref.at[b], coords_ref.at[b], weights_ref.at[pl.ds(b, 1)], metric_ref.at[b])
+            load(b).wait()
+
+            @pl.when(b + 1 < batches)
+            def _():
+                load(b + 1).start()
+
+            metric_kernel(colloc_ref.at[lax.rem(b, 2)], coords_ref.at[b], weights_ref.at[pl.ds(b, 1)], metric_ref.at[b])
             return carry
 
         lax.fori_loop(first, last, one, 0)
@@ -338,8 +491,10 @@
     scalars.start()
     scalars.wait()
     serve(0)
-    slot_tables(asked_ref, tables_ref, line, capacity)
-    load.wait()
+    slot_tables(asked_ref, tables_vmem, line, capacity)
+    scalars = pltpu.make_async_copy(tables_vmem, tables_ref, smem_sem)
+    scalars.start()
+    scalars.wait()
     for d in range(1, line):
         metrics(batches * (d - 1) // (line - 1), batches * d // (line - 1))
         if 2 * d == line:
@@ -380,49 +535,47 @@
 
     lax.fori_loop(0, batches // buffers, products, 0)
 
-    def put_out(source):
-        return pltpu.make_async_copy(
-            stage.at[source], outgoing_ref.at[pl.ds(source * plane, plane)], out_sem.at[source]
-        )
-
-    for source in range(line):
-
-        def arrange(lane, carry):
+    def arrange(source):
+        def one(lane, carry):
             for r in range(capacity):
                 stage[source, lane, r] = parts_ref[inverse_ref[(source * plane + lane) * capacity + r]]
             return carry
 
-        lax.fori_loop(0, plane, arrange, 0)
-        put_out(source).start()
-    for source in range(line):
-        put_out(source).wait()
-
-
-def fetch(wanted, scales, pos, inverse, counts, dens, collocation, coords, weights, plane, line, capacity):
+        lax.fori_loop(0, plane, one, 0)
+
+    give_back(
+        z, q, plane, line, arrange, tables_ref, stage, prev_ref, out_ref, received, pools[1:], running, inbox, *return_sems
+    )
+
+
+def exchange(
+    wanted, scales, pos, inverse, counts, dens, collocation, coords, weights, prev, plane, line, capacity
+):
     stored, width, _ = dens.shape
     per_dev, points, funcs = collocation.shape
     vmem, smem = pl.BlockSpec(memory_space=pltpu.VMEM), pl.BlockSpec(memory_space=pltpu.SMEM)
     hbm = pl.BlockSpec(memory_space=pl.ANY)
     return pl.pallas_call(
-        functools.partial(fetch_kernel, plane, line),
-        out_shape=(
-            jax.ShapeDtypeStruct((line * plane, capacity, width, width), jnp.bfloat16),
-            jax.ShapeDtypeStruct((line, 8, plane * capacity), jnp.int32),
-        ),
-        in_specs=[vmem, smem, smem, smem, smem, vmem, hbm, vmem, vmem],
-        out_specs=(hbm, vmem),
+        functools.partial(exchange_kernel, plane, line),
+        out_shape=jax.ShapeDtypeStruct(prev.shape, jnp.float32),
+        in_specs=[vmem, smem, smem, smem, smem, vmem, hbm, vmem, vmem, vmem],
+        out_specs=vmem,
         scratch_shapes=[pltpu.VMEM((stored, width, width), jnp.bfloat16)] * line
+        + [pltpu.VMEM((plane * capacity, width, width), jnp.bfloat16)] * line
         + [
             pltpu.VMEM((line, plane, capacity, width, width), jnp.bfloat16),
             pltpu.VMEM((line * plane * capacity, width, width), jnp.bfloat16),
-            pltpu.VMEM((line * plane * capacity, width, width), jnp.bfloat16),
             pltpu.VMEM((2 - per_dev % 2, funcs, funcs), jnp.bfloat16),
-            pltpu.VMEM((per_dev, points, funcs), jnp.bfloat16),
+            pltpu.VMEM((2, points, funcs), jnp.bfloat16),
             pltpu.VMEM((per_dev, funcs, funcs), jnp.bfloat16),
             pltpu.VMEM(wanted.shape, jnp.int32),
             pltpu.SMEM(wanted.shape, jnp.int32),
-            pltpu.SemaphoreType.DMA,
-            pltpu.SemaphoreType.DMA((line,)),
+            pltpu.VMEM((line, 8, plane * capacity), jnp.int32),
+            pltpu.SMEM((line, 8, plane * capacity), jnp.int32),
+            pltpu.VMEM((plane * capacity, width, width), jnp.float32),
+            pltpu.VMEM((line + 1, stored, width, width), jnp.bfloat16),
+            pltpu.VMEM((line * plane * capacity, width, width), jnp.bfloat16),
+            pltpu.SemaphoreType.DMA((2,)),
             pltpu.SemaphoreType.DMA,
             pltpu.SemaphoreType.DMA((plane,)),
             pltpu.SemaphoreType.DMA((plane,)),
@@ -431,172 +584,6 @@
             pltpu.SemaphoreType.DMA((line,)),
             pltpu.SemaphoreType.DMA((line, plane)),
             pltpu.SemaphoreType.DMA((line, plane)),
-        ],
-        compiler_params=pltpu.CompilerParams(
-            collective_id=0, has_side_effects=True, vmem_limit_bytes=VMEM_BYTES
-        ),
-        name="fetch",
-    )(wanted, scales, pos, inverse, counts, dens, collocation, coords, weights)
-
-
-def return_kernel(
-    plane, line, tables_ref, outgoing_ref, prev_ref, out_ref, *scratch
-):
-    received, rest = scratch[:line], scratch[line:]
-    running, part, inbox, hop_send, hop_recv, local_sem, send_sem, recv_sem = rest
-    capacity = outgoing_ref.shape[1]
-    stored, width, _ = prev_ref.shape
-    entries = plane * capacity
-    me = lax.axis_index("grid")
-    z, q = me // plane, lax.rem(me, plane)
-    order = [jnp.where(z == 0, line - 1 - p, jnp.where(z == line - 1, (p + 1) % line, (2, 1, 3, 0)[p])) for p in range(line)]
-    greet(z, q, plane, line)
-
-    def to_mate(p, k):
-        to = lax.rem(q + k, plane)
-        return pltpu.make_async_remote_copy(
-            src_ref=outgoing_ref.at[lax.rem(z + order[p], line) * plane + to],
-            dst_ref=received[p].at[pl.ds(q * capacity, capacity)],
-            send_sem=send_sem.at[p, k],
-            recv_sem=recv_sem.at[p, k],
-            device_id=mate(z, to, plane),
-            device_id_type=pl.DeviceIdType.MESH,
-        )
-
-    def to_self(p):
-        return pltpu.make_async_copy(
-            outgoing_ref.at[lax.rem(z + order[p], line) * plane + q],
-            received[p].at[pl.ds(q * capacity, capacity)],
-            local_sem.at[p],
-        )
-
-    def exchange(p):
-        def one(k, carry):
-            to_mate(p, k).start()
-            return carry
-
-        lax.fori_loop(1, plane, one, 0)
-        to_self(p).start()
-
-    def hop(p, up):
-        to = order[p] - 1 if up else order[p] + 1
-        return pltpu.make_async_remote_copy(
-            src_ref=part.at[p],
-            dst_ref=inbox.at[to],
-            send_sem=hop_send.at[p],
-            recv_sem=hop_recv.at[to],
-            device_id=mate(z + 1 if up else z - 1, q, plane),
-            device_id_type=pl.DeviceIdType.MESH,
-        )
-
-    def arrival(slot):
-        return pltpu.make_async_remote_copy(
-            src_ref=part.at[0],
-            dst_ref=inbox.at[slot],
-            send_sem=hop_send.at[0],
-            recv_sem=hop_recv.at[slot],
-            device_id=mate(z, lax.rem(q + 1, plane), plane),
-            device_id_type=pl.DeviceIdType.MESH,
-        )
-
-    def gather(p):
-        def finish(k, carry):
-            to_mate(p, k).wait()
-            return carry
-
-        lax.fori_loop(1, plane, finish, 0)
-        to_self(p).wait()
-        if p + 2 < line:
-            exchange(p + 2)
-        row = lax.rem(z + order[p], line)
-
-        def one(k, total):
-            tile = received[p][tables_ref[row, 0, k]].astype(jnp.float32)
-            total = jnp.where(tables_ref[row, 1, k] != 0, total, 0.0) + tile
-            running[k] = total
-            return total
-
-        lax.fori_loop(0, entries, one, jnp.zeros((width, width), jnp.float32), unroll=4)
-
-    def slot_sum(p, t):
-        row = lax.rem(z + order[p], line)
-        return jnp.where(tables_ref[row, 3, t] != 0, running[tables_ref[row, 2, t]], 0.0)
-
-    def each(body):
-        def one(t, carry):
-            body(t)
-            return carry
-
-        lax.fori_loop(0, stored, one, 0, unroll=4)
-
-    exchange(0)
-    exchange(1)
-    for p in range(line - 1):
-        gather(p)
-        up = z + order[p] < line
-        feeds = jnp.where(up, z > 0, z < line - 1)
-
-        @pl.when(feeds)
-        def _():
-            arrival(order[p]).wait_recv()
-
-            def body(t):
-                part[p, t] = (slot_sum(p, t) + inbox[order[p], t].astype(jnp.float32)).astype(jnp.bfloat16)
-
-            each(body)
-
-        @pl.when(jnp.logical_not(feeds))
-        def _():
-            def body(t):
-                part[p, t] = slot_sum(p, t).astype(jnp.bfloat16)
-
-            each(body)
-
-        pl.when(up)(lambda: hop(p, True).start())
-        pl.when(jnp.logical_not(up))(lambda: hop(p, False).start())
-    gather(line - 1)
-
-    def first(t):
-        out_ref[t] = prev_ref[t].astype(jnp.float32) - 0.5 * slot_sum(line - 1, t)
-
-    each(first)
-    for slot, there in ((0, z > 0), (line, z < line - 1)):
-
-        @pl.when(there)
-        def _():
-            arrival(slot).wait_recv()
-
-            def body(t):
-                out_ref[t] = out_ref[t] - 0.5 * inbox[slot, t].astype(jnp.float32)
-
-            each(body)
-
-    for p in range(line - 1):
-        arrival_of = pltpu.make_async_remote_copy(
-            src_ref=part.at[p],
-            dst_ref=inbox.at[0],
-            send_sem=hop_send.at[p],
-            recv_sem=hop_recv.at[0],
-            device_id=mate(z, lax.rem(q + 1, plane), plane),
-            device_id_type=pl.DeviceIdType.MESH,
-        )
-        arrival_of.wait_send()
-
-
-def give_back(tables, outgoing, prev, plane, line):
-    stored, width, _ = prev.shape
-    capacity = outgoing.shape[1]
-    vmem, smem = pl.BlockSpec(memory_space=pltpu.VMEM), pl.BlockSpec(memory_space=pltpu.SMEM)
-    return pl.pallas_call(
-        functools.partial(return_kernel, plane, line),
-        out_shape=jax.ShapeDtypeStruct((stored, width, width), jnp.float32),
-        in_specs=[smem, pl.BlockSpec(memory_space=pl.ANY), vmem],
-        out_specs=vmem,
-        scratch_shapes=[pltpu.VMEM((plane * capacity, width, width), jnp.bfloat16)] * line
-        + [
-            pltpu.VMEM((plane * capacity, width, width), jnp.float32),
-            pltpu.VMEM((line - 1, stored, width, width), jnp.bfloat16),
-            pltpu.VMEM((line + 1, stored, width, width), jnp.bfloat16),
             pltpu.SemaphoreType.DMA((line - 1,)),
             pltpu.SemaphoreType.DMA((line + 1,)),
             pltpu.SemaphoreType.DMA((line,)),
@@ -604,10 +591,10 @@
             pltpu.SemaphoreType.DMA((line, plane)),
         ],
         compiler_params=pltpu.CompilerParams(
-            collective_id=1, has_side_effects=True, vmem_limit_bytes=VMEM_BYTES
+            collective_id=0, has_side_effects=True, vmem_limit_bytes=VMEM_BYTES
         ),
-        name="give_back",
-    )(tables, outgoing, prev)
+        name="exchange",
+    )(wanted, scales, pos, inverse, counts, dens, collocation, coords, weights, prev)
 
 
 def shards(collocation, coords, weights, owners, slots, counts, dens_tiles, dens_scales, fock_prev):
@@ -639,11 +626,10 @@
         inverse = jnp.dot(
             onehot.T.astype(jnp.float32), numbered.astype(jnp.float32), precision=lax.Precision.HIGHEST
         ).astype(jnp.int32)
-        outgoing, tables = fetch(
+        return exchange(
             wanted, dens_scales, pos, inverse.reshape(-1), counts, dens_tiles, collocation, coords, weights,
-            plane, line, capacity,
-        )
-        return give_back(tables, outgoing, fock_prev, plane, line)
+            fock_prev, plane, line, capacity,
+        )
     asked = lax.all_to_all(requests, "grid", split_axis=0, concat_axis=0, tiled=True).reshape(-1)
     chunk = 16
     tiles = pick(asked, dens_scales, dens_tiles, chunk)

time: 227 us -> 218 us (0.960); the launches traced: 227 us -> 216 us
  Pallas kernels: 218 us -> 206 us
    pallas_call x2 -> x1, Pallas kernels: 218 us -> 206 us  [exchange(): pl.pallas_call(functools.partial(exchange_kernel, plane, line), out_shape...]
where the time goes in v5:
time: 218 us; the launch traced here: 216 us
  Pallas kernels  206 us (94%)
  local copies, waits for them, and re-layouts  7.89 us (4%)
    pallas_call x1, Pallas kernels, exchange(): pl.pallas_call(functools.partial(exchange_kernel, plane, line), out_shape...  206 us
    unnamed x2, local copies, waits for them, and re-layouts  4.75 us

profile of v5, /device:TPU:0, one launch (start us, length us, event | category | flops | bytes accessed | tf_op | source)
XLA Modules:
  0.0 215.8 jit_solution(2672461901265736052)
XLA Ops:
  0.0 0.8 eq.14
  0.8 0.8 broadcast_in_dim.35
  1.6 0.3 fusion
  1.8 0.6 multiply_add_fusion.pos_ref
  2.4 0.3 convolution_convert_fusion.1
  2.7 0.3 convolution_convert_fusion
  3.0 0.1 copy.13
  3.1 0.6 reshape.17.inverse_ref
  3.8 0.1 reshape.15
  3.8 0.1 copy.12
  3.9 0.1 reshape.16
  4.0 0.6 pad.4.wanted_ref
  4.6 1.6 copy.14.coords_ref
  6.2 206.4 %exchange.1 = f32[32,128,128]{2,1,0:T(8,128)} custom-call(s32[8,8,128]{2,1,0:T(8,128)} %pad.4.wanted_ref, f32[32]{0:T(128)} %scales_ref.1, s32[256]{0:T(256)} %multiply_add_fusion.pos_ref, s32[256]{0:T(256)} %reshape.17.inverse_ref, s32[16]{0:T(128)} %counts_ref.1, bf16[32,128,128]{2,1,0:T(8,128)(2,1)} %dens_ref.1, bf16[16,512,512]{2,1,0:T(8,128)(2,1)} %colloc_hbm.1, ...), custom_call_target="tpu_custom_call" | custom-call | tf_op jit(solution)/shard_map/exchange/pallas_call | solution.py:558
  212.7 3.1 %copy.16 = f32[32,128,128]{2,1,0:T(8,128)} copy(f32[32,128,128]{2,1,0:T(8,128)} %exchange.1) | data formatting | bytes 4194304
  (2 shorter events, 0.0 us)

commit v6 on v5

--- a/solution.py
+++ b/solution.py
@@ -227,7 +227,7 @@
 
 def give_back(
     z, q, plane, line, arrange, tables_ref, stage, prev_ref, out_ref, received, part, running, inbox,
-    hop_send, hop_recv, local_sem, send_sem, recv_sem
+    hop_send, hop_recv, local_sem, send_sem, recv_sem, out_hbm, out_sem
 ):
     capacity, width = stage.shape[2:4]
     stored = prev_ref.shape[0]
@@ -354,7 +354,17 @@
         total = slot_sum(line - 1, t) + inbox[0, t].astype(jnp.float32) + inbox[line, t].astype(jnp.float32)
         out_ref[t] = prev_ref[t].astype(jnp.float32) - 0.5 * total
 
-    each(last)
+    halves = [pl.ds(h * (stored // 2), stored // 2) for h in range(2)]
+    for h, rows in enumerate(halves):
+
+        def some(t, carry):
+            last(h * (stored // 2) + t)
+            return carry
+
+        lax.fori_loop(0, stored // 2, some, 0, unroll=4)
+        pltpu.make_async_copy(out_ref.at[rows], out_hbm.at[rows], out_sem.at[h]).start()
+    for h, rows in enumerate(halves):
+        pltpu.make_async_copy(out_ref.at[rows], out_hbm.at[rows], out_sem.at[h]).wait()
     for p in range(line - 1):
         arrival_of = pltpu.make_async_remote_copy(
             src_ref=part[p],
@@ -369,13 +379,13 @@
 
 def exchange_kernel(
     plane, line, wanted_ref, scales_ref, pos_ref, inverse_ref, counts_ref, dens_ref, colloc_hbm, coords_ref,
-    weights_ref, prev_ref, out_ref, *scratch
+    weights_ref, prev_ref, out_hbm, *scratch
 ):
     pools, received, rest = scratch[:line], scratch[line : 2 * line], scratch[2 * line :]
     stage, fetched_ref, dmat_ref, colloc_ref, metric_ref, asked_vmem, asked_ref, tables_vmem, tables_ref = rest[:9]
-    running, inbox, parts_ref = rest[9:12]
-    in_sem, smem_sem, ask_send, ask_recv, hop_send, hop_recv, local_sem, send_sem, recv_sem = rest[12:21]
-    return_sems = rest[21:]
+    running, inbox, parts_ref, out_ref, out_sem = rest[9:14]
+    in_sem, smem_sem, ask_send, ask_recv, hop_send, hop_recv, local_sem, send_sem, recv_sem = rest[14:23]
+    return_sems = rest[23:]
     capacity, width = stage.shape[2:4]
     listed = colloc_hbm.shape[2] // width
     stored = dens_ref.shape[0]
@@ -544,7 +554,8 @@
         lax.fori_loop(0, plane, one, 0)
 
     give_back(
-        z, q, plane, line, arrange, tables_ref, stage, prev_ref, out_ref, received, pools[1:], running, inbox, *return_sems
+        z, q, plane, line, arrange, tables_ref, stage, prev_ref, out_ref, received, pools[1:], running, inbox, *return_sems,
+        out_hbm, out_sem
     )
 
 
@@ -559,7 +570,7 @@
         functools.partial(exchange_kernel, plane, line),
         out_shape=jax.ShapeDtypeStruct(prev.shape, jnp.float32),
         in_specs=[vmem, smem, smem, smem, smem, vmem, hbm, vmem, vmem, vmem],
-        out_specs=vmem,
+        out_specs=hbm,
         scratch_shapes=[pltpu.VMEM((stored, width, width), jnp.bfloat16)] * line
         + [pltpu.VMEM((plane * capacity, width, width), jnp.bfloat16)] * line
         + [
@@ -575,6 +586,8 @@
             pltpu.VMEM((plane * capacity, width, width), jnp.float32),
             pltpu.VMEM((line + 1, stored, width, width), jnp.bfloat16),
             pltpu.VMEM((line * plane * capacity, width, width), jnp.bfloat16),
+            pltpu.VMEM((stored, width, width), jnp.float32),
+            pltpu.SemaphoreType.DMA((2,)),
             pltpu.SemaphoreType.DMA((2,)),
             pltpu.SemaphoreType.DMA,
             pltpu.SemaphoreType.DMA((plane,)),
@@ -606,9 +619,10 @@
     flat_owner = owners.reshape(-1)
     flat_slot = slots.reshape(-1)
     onehot = (flat_owner[:, None] == jnp.arange(npeer, dtype=jnp.int32)[None, :]).astype(jnp.bfloat16)
-    before = jnp.tril(jnp.ones((entries, entries), jnp.bfloat16), -1)
-    running = jnp.dot(before, onehot, preferred_element_type=jnp.float32)
-    rank = jnp.sum(running * onehot.astype(jnp.float32), axis=1).astype(jnp.int32)
+    batch = jnp.arange(per_dev, dtype=jnp.int32)
+    named = jnp.sum(onehot.reshape(per_dev, npair, npeer).astype(jnp.float32), axis=1)
+    running = jnp.sum(jnp.where((batch[None, :] < batch[:, None])[:, :, None], named[None], 0.0), axis=1)
+    rank = jnp.sum(onehot.reshape(per_dev, npair, npeer) * running[:, None, :], axis=2).reshape(-1).astype(jnp.int32)
     pos = flat_owner * capacity + rank
     ranked = jnp.where(
         rank[:, None] == jnp.arange(capacity, dtype=jnp.int32)[None, :], flat_slot[:, None], 0

time: 218 us -> 219 us (level)
  no operation moved by 1% of the time
where the time goes in v6:
time: 219 us; the launch traced here: 217 us
  Pallas kernels  206 us (94%)
  local copies, waits for them, and re-layouts  7.96 us (4%)
  other arithmetic  2.33 us (1%)
    pallas_call x1, Pallas kernels, exchange(): pl.pallas_call(functools.partial(exchange_kernel, plane, line), out_shape...  206 us
    unnamed x2, local copies, waits for them, and re-layouts  4.75 us

profile of v6, /device:TPU:0, one launch (start us, length us, event | category | flops | bytes accessed | tf_op | source)
XLA Modules:
  0.0 217.1 jit_solution(5406664705328795753)
XLA Ops:
  0.0 0.8 eq.42
  0.8 0.8 broadcast_in_dim.54
  1.6 0.8 convert_reduce_fusion
  2.4 0.9 fusion.20
  3.3 0.1 convert_element_type.34
  3.4 0.6 multiply_add_fusion.pos_ref
  4.0 0.3 convolution_convert_fusion.1
  4.3 0.3 convolution_convert_fusion
  4.6 0.1 copy.16
  4.7 0.6 reshape.45.inverse_ref
  5.3 0.1 reshape.43
  5.4 0.1 copy.15
  5.5 0.1 reshape.44
  5.6 0.6 pad.4.wanted_ref
  6.2 1.6 copy.17.coords_ref
  7.8 206.2 %exchange.1 = f32[32,128,128]{2,1,0:T(8,128)} custom-call(s32[8,8,128]{2,1,0:T(8,128)} %pad.4.wanted_ref, f32[32]{0:T(128)} %scales_ref.1, s32[256]{0:T(256)} %multiply_add_fusion.pos_ref, s32[256]{0:T(256)} %reshape.45.inverse_ref, s32[16]{0:T(128)} %counts_ref.1, bf16[32,128,128]{2,1,0:T(8,128)(2,1)} %dens_ref.1, bf16[16,512,512]{2,1,0:T(8,128)(2,1)} %colloc_hbm.1, ...), custom_call_target="tpu_custom_call" | custom-call | tf_op jit(solution)/shard_map/exchange/pallas_call | solution.py:569
  214.0 3.1 %copy.19 = f32[32,128,128]{2,1,0:T(8,128)} copy(f32[32,128,128]{2,1,0:T(8,128)} %exchange.1) | data formatting | bytes 4194304
  (2 shorter events, 0.0 us)
